TPU v7x, 32 devices: a whole 2x2x4 slice. The times are simulated.
32 devices in a mesh: fsdp: 8 (over z, x), tp: 4 (over y, core).
Axes of the slice: x: 2, y: 2, z: 4, core: 2. Of those that a mesh axis runs over, the one named last changes fastest.
Arguments:
- tokens: bfloat16 [2, 1024, 2048], P(None, 'fsdp'), may hold values from -6 to 6
- cotangent: bfloat16 [2, 1024, 2048], P(None, 'fsdp'), may hold values from -6 to 6
- expert_ids: int32 [2, 1024, 8], P(None, 'fsdp'), may hold values from 0 to 31, all different within a row; in each aligned block of 128 rows (0 to 127, 128 to 255, ..., all dimensions but the last counted through in order) at most 40 rows name the same one
- attention_gain: float32 [2048], replicated, may hold values from 0.5 to 1.5
- query_gain: float32 [128], replicated, may hold values from 0.5 to 1.5
- key_gain: float32 [128], replicated, may hold values from 0.5 to 1.5
- query_weight: bfloat16 [2048, 4096], P('fsdp', 'tp'), may hold values from -0.125 to 0.125
- key_weight: bfloat16 [2048, 512], P('fsdp', 'tp'), may hold values from -0.125 to 0.125
- value_weight: bfloat16 [2048, 512], P('fsdp', 'tp'), may hold values from -0.125 to 0.125
- output_weight: bfloat16 [2048, 4096], P('fsdp', 'tp'), may hold values from -0.75 to 0.75
- expert_gain: float32 [2048], replicated, may hold values from 0.5 to 1.5
- router_weight: bfloat16 [2048, 32], P('fsdp'), may hold values from -0.0625 to 0.0625
- gate_weight: bfloat16 [32, 768, 2048], P('fsdp', 'tp'), may hold values from -0.125 to 0.125
- up_weight: bfloat16 [32, 768, 2048], P('fsdp', 'tp'), may hold values from -0.125 to 0.125
- down_weight: bfloat16 [32, 768, 2048], P('fsdp', 'tp'), may hold values from -0.875 to 0.875
Outputs:
- layer_output: bfloat16 [2, 1024, 2048], P(None, 'fsdp')
- tokens_gradient: bfloat16 [2, 1024, 2048], P(None, 'fsdp')
- attention_gain_gradient: float32 [2048], P('fsdp')
- query_gain_gradient: float32 [128], P('fsdp')
- key_gain_gradient: float32 [128], P('fsdp')
- query_weight_gradient: float32 [2048, 4096], P('fsdp', 'tp')
- key_weight_gradient: float32 [2048, 512], P('fsdp', 'tp')
- value_weight_gradient: float32 [2048, 512], P('fsdp', 'tp')
- output_weight_gradient: float32 [2048, 4096], P('fsdp', 'tp')
- expert_gain_gradient: float32 [2048], P('fsdp')
- router_weight_gradient: float32 [2048, 32], P('fsdp')
- gate_weight_gradient: float32 [32, 768, 2048], P('fsdp', 'tp')
- up_weight_gradient: float32 [32, 768, 2048], P('fsdp', 'tp')
- down_weight_gradient: float32 [32, 768, 2048], P('fsdp', 'tp')
Inputs may be any that keep to these rules, and one draw needn't show every extreme that they name: `expert_ids`: each row names 8 different experts. Among the 128 tokens of one micro-batch on one index of fsdp (aligned blocks of 128 rows), no expert is named more than 40 times, and in some such block some expert is named exactly 40 times.
All inputs are finite; a program needn't handle non-finite values.
Results may differ from a plain program's by a relative error of at most 0.029.
Values may be sent and summed in bfloat16 or wider, within the bound.
A program may use at most 256 MiB of HBM per device.

v0:
```python
import functools
import math

import jax
import jax.numpy as jnp
import numpy as np
from jax import lax
from jax.experimental import pallas as pl
from jax.experimental.pallas import tpu as pltpu
from jax.sharding import PartitionSpec as P

norm_eps = 1e-06
rope_base = 1000000.0
masked_score = -1e30
MESH = pl.DeviceIdType.MESH
LOW = jnp.bfloat16
F32 = jnp.float32
VMEM_LIMIT = 60 * 2**20


def coords():
    f = lax.axis_index("fsdp")
    t = lax.axis_index("tp")
    return f // 2, f % 2, t // 2, t % 2


def place(z, x, y, c):
    return (2 * z + x, 2 * y + c)


def span(first, count):
    return pl.ds(pl.multiple_of(first, count), count)


class Here:
    def __init__(self):
        z, x, y, c = coords()
        self.z, self.x, self.y, self.c = z, x, y, c
        self.f, self.t = 2 * z + x, 2 * y + c
        self.xn, self.yn, self.cn = place(z, 1 - x, y, c), place(z, x, 1 - y, c), place(z, x, y, 1 - c)
        self.lanes = ((x, y), (1 - x, y), (x, 1 - y), (1 - x, 1 - y))

    def zr(self, d):
        return (self.z + d) % 4

    def flip(self, k):
        return (self.z // 2 + k // 2) % 2 * 2 + (self.z % 2 + k % 2) % 2

    def zd(self, j):
        inner = (self.z % 3 + 1) // 2
        return self.flip(j + inner * (j // 2) * (1 - 2 * (j % 2)))

    def at_z(self, z):
        return place(z, self.x, self.y, self.c)

    def number(self, j, e):
        return 2 * self.zd(j) + (self.x + e) % 2

    def peer(self, d, e):
        return place(self.zr(d), (self.x + e) % 2, self.y, self.c)

    def greet(self):
        barrier = pltpu.get_barrier_semaphore()
        peers = [self.peer(d, e) for d in range(4) for e in range(2) if d or e] + [self.yn, self.cn]
        for peer in peers:
            pl.semaphore_signal(barrier, inc=1, device_id=peer, device_id_type=MESH)
        pl.semaphore_wait(barrier, len(peers))


def remote(src, dst, send_sem, recv_sem, device):
    return pltpu.make_async_remote_copy(
        src_ref=src, dst_ref=dst, send_sem=send_sem, recv_sem=recv_sem, device_id=device, device_id_type=MESH
    )


def push(src, dst, send_sem, recv_sem, device):
    copy = remote(src, dst, send_sem, recv_sem, device)
    copy.start()
    return copy


def keep(src, dst, sem):
    copy = pltpu.make_async_copy(src, dst, sem)
    copy.start()
    return copy


ORDER = (1, 2, 3)
FAR_FIRST = (3, 2, 1, 0)


class Gather:
    scratch = staticmethod(
        lambda: [pltpu.SemaphoreType.DMA((1,)), pltpu.SemaphoreType.DMA((6,))]
        + [pltpu.SemaphoreType.DMA((4,))] * 9
        + [pltpu.SemaphoreType.DMA((4, 4))] * 2
    )
    slots = 13

    def __init__(self, here, whole, src, dst, sems, by_x, own=None):
        self.here, self.whole, self.src, self.dst, self.own_rows = here, whole, src, dst, own
        (self.loc, self.sz, self.rz, self.sx, self.rx, self.sy, self.ry,
         self.sdx, self.rdx, self.sdy, self.rdy, self.sc, self.rc) = sems
        self.rows, self.cols = src.shape[1], src.shape[2] // 4
        self.half = by_x
        self.sends = []

    def block(self, z, x, y, c, h=None):
        first = (2 * z + x) * self.rows
        rows = span(first, self.rows)
        if h is not None:
            start, count = ((0, self.half), (self.half, self.rows - self.half))[h]
            rows = pl.ds(pl.multiple_of(first + start, 16), count)
        return self.dst.at[:, rows, span((2 * y + c) * self.cols, self.cols)]

    def source(self, z_to, t, first, count):
        seqs = slice(None) if self.whole else pl.ds(z_to // 2, 1)
        return self.src.at[seqs, pl.ds(first, count), span(t * self.cols, self.cols)]

    def push(self, make, when=None):
        if when is None:
            push(*make())
        else:
            pl.when(when)(lambda: push(*make()) and None)
        self.sends.append((make, when))

    def landed(self, ref, sem):
        pltpu.make_async_remote_copy(
            src_ref=ref, dst_ref=ref, send_sem=sem, recv_sem=sem, device_id=self.here.xn, device_id_type=MESH
        ).wait_recv()

    def start(self):
        h = self.here
        self.inner = h.z % 3 > 0
        self.along(0, h.flip(1), True)
        self.along(1, h.flip(3), self.inner)
        if not self.whole:
            self.along(2, h.flip(2), h.z % 3 == 0)
        self.push(lambda: (self.source(h.z, h.t, 0, self.rows), self.block(h.z, h.x, h.y, h.c),
                           self.sx.at[h.z], self.rx.at[h.z], h.xn))
        if self.half:
            self.push(lambda: (self.source(h.z, 2 * (1 - h.y) + h.c, 0, self.half),
                               self.block(h.z, h.x, 1 - h.y, h.c, 0), self.sdx.at[h.z], self.rdx.at[h.z], h.xn))
        own = self.src if self.whole else self.src.at[pl.ds(h.z // 2, 1)]
        if self.own_rows is not None:
            own = self.own_rows
            pltpu.make_async_copy(self.src, own, self.loc.at[0]).start()
            pltpu.make_async_copy(self.src, own, self.loc.at[0]).wait()
        self.own = keep(own, self.dst.at[:, span(h.f * self.rows, self.rows), :], self.loc.at[0])

    def along(self, n, z_to, when):
        h = self.here
        self.push(lambda: (self.source(z_to, h.t, 0, self.rows), self.block(h.z, h.x, h.y, h.c),
                           self.sz.at[n], self.rz.at[h.z], h.at_z(z_to)), None if when is True else when)

    def relay(self, j):
        h, zd = self.here, self.here.zd(j)
        self.landed(self.block(zd, h.x, h.y, h.c), self.rz.at[zd])
        if j > 1 or self.whole:

            def make():
                b = self.block(h.zd(j), h.x, h.y, h.c)
                return b, b, self.sz.at[2 + j], self.rz.at[h.zd(j)], h.at_z(h.flip(3 if j == 1 else 1))

            self.push(make, self.inner)

    def pass_on(self, d, lane, sends, recvs, device, h=None):
        x, y = self.here.lanes[lane]

        def make():
            zd = self.here.zd(d)
            b = self.block(zd, x, y, self.here.c, h)
            return b, b, sends(zd), recvs(zd), device

        self.push(make)

    def spread(self, d):
        h = self.here
        self.pass_on(d, 0, lambda k: self.sx.at[k], lambda k: self.rx.at[k], h.xn)
        self.pass_on(d, 0, lambda k: self.sy.at[k], lambda k: self.ry.at[k], h.yn)
        self.pass_on(d, 0, lambda k: self.sc.at[0, k], lambda k: self.rc.at[0, k], h.cn)

    def cross(self, d):
        h, zd = self.here, self.here.zd(d)
        self.landed(self.block(zd, 1 - h.x, h.y, h.c), self.rx.at[zd])
        self.pass_on(d, 1, lambda k: self.sdy.at[k], lambda k: self.rdy.at[k], h.yn, 1)
        self.pass_on(d, 1, lambda k: self.sc.at[1, k], lambda k: self.rc.at[1, k], h.cn)
        if d != 0:
            self.landed(self.block(zd, h.x, 1 - h.y, h.c), self.ry.at[zd])
            if self.half:
                self.pass_on(d, 2, lambda k: self.sdx.at[k], lambda k: self.rdx.at[k], h.xn, 0)
            self.pass_on(d, 2, lambda k: self.sc.at[2, k], lambda k: self.rc.at[2, k], h.cn)

    def close(self, d):
        h, zd = self.here, self.here.zd(d)
        if self.half:
            self.landed(self.block(zd, 1 - h.x, 1 - h.y, h.c, 0), self.rdx.at[zd])
        self.landed(self.block(zd, 1 - h.x, 1 - h.y, h.c, 1), self.rdy.at[zd])
        self.pass_on(d, 3, lambda k: self.sc.at[3, k], lambda k: self.rc.at[3, k], h.cn)

    def first_steps(self):
        for j in ORDER:
            self.relay(j)
            self.spread(j)
            if j < 3:
                self.cross(j - 1)

    def last_steps(self):
        self.close(0)
        for j in (2, 3):
            self.cross(j)
            self.close(j - 1)
        self.close(3)

    def arrived(self, d, e):
        h, zd = self.here, self.here.zd(d)
        if e == 0:
            if d == 0:
                self.own.wait()
            else:
                self.landed(self.block(zd, h.x, h.y, 1 - h.c), self.rc.at[0, zd])
                self.landed(self.block(zd, h.x, 1 - h.y, 1 - h.c), self.rc.at[2, zd])
        else:
            self.landed(self.block(zd, 1 - h.x, h.y, 1 - h.c), self.rc.at[1, zd])
            self.landed(self.block(zd, 1 - h.x, 1 - h.y, 1 - h.c), self.rc.at[3, zd])

    def finish(self):
        for make, when in self.sends:
            if when is None:
                remote(*make()).wait_send()
            else:
                pl.when(when)(lambda make=make: remote(*make()).wait_send())


def add_into(target, *others):
    count, rows, _ = target.shape
    step = 32

    @pl.loop(0, count * rows // step)
    def _(i):
        n = i // (rows // step)
        r = pl.ds(pl.multiple_of((i % (rows // step)) * step, step), step)
        total = target[n, r, :].astype(F32)
        for other in others:
            total = total + other[n, r, :].astype(F32)
        target[n, r, :] = total.astype(target.dtype)


class Sum:
    slots = 23

    @staticmethod
    def scratch(count, rows, width, low, by_x):
        dma = pltpu.SemaphoreType.DMA
        cols = width // 4
        vm = pltpu.VMEM
        return [
            vm((4, 4, count, rows, cols), low),
            vm((4, count, max(by_x, 16), cols), low),
            vm((4, count, rows - by_x, cols), low),
            vm((4, count, rows, cols), low),
            vm((4, count, rows, cols), low),
            vm((4, count, rows, cols), low),
            vm((4, 2, rows, cols), low),
            vm((2, rows, cols), low),
            dma((4, 4)), dma((4, 4)),
        ] + [dma((4,))] * 10 + [dma((3,))] * 2 + [dma((5,))]

    def __init__(self, here, whole, part, refs, by_x):
        self.here, self.whole, self.part, self.by_x = here, whole, part, by_x
        (self.fc, self.f1x, self.f1y, self.f2x, self.f2y, self.fz, self.full, self.tmp, self.sc, self.rc,
         self.s1x, self.r1x, self.s1y, self.r1y, self.s2x, self.r2x, self.s2y, self.r2y, self.sz, self.rz,
         self.sg, self.rg, self.osem) = refs
        self.rows, self.cols = part.shape[1] // 8, part.shape[2] // 4
        self.top, self.low = pl.ds(0, by_x), pl.ds(by_x, self.rows - by_x)
        self.sends = []

    def block(self, d, lane, c):
        x, y = self.here.lanes[lane]
        return self.part.at[:, span((2 * self.here.zd(d) + x) * self.rows, self.rows),
                            span((2 * y + c) * self.cols, self.cols)]

    def push(self, make):
        push(*make())
        self.sends.append(make)

    def landed(self, ref, sem):
        pltpu.make_async_remote_copy(
            src_ref=ref, dst_ref=ref, send_sem=sem, recv_sem=sem, device_id=self.here.xn, device_id_type=MESH
        ).wait_recv()

    def giving(self, d, e):
        h = self.here
        for q in (0, 1):
            lane = 2 * q + e
            at = self.part.at[:, span((2 * h.zd(d) + (h.x + e) % 2) * self.rows, self.rows),
                              span((2 * ((h.y + q) % 2) + 1 - h.c) * self.cols, self.cols)]
            yield at, self.fc.at[lane, d], self.sc.at[lane, d], self.rc.at[lane, d], h.cn

    def give(self, d, e):
        for args in self.giving(d, e):
            push(*args)

    def pair(self, lane, d):
        self.landed(self.fc.at[lane, d], self.rc.at[lane, d])
        add_into(self.block(d, lane, self.here.c), self.fc.at[lane, d])

    def mine(self, d, lane, rows=slice(None)):
        return self.block(d, lane, self.here.c).at[:, rows]

    def corner(self, d):
        self.pair(3, d)
        if self.by_x:
            self.push(lambda: (self.mine(d, 3, self.top), self.f1x.at[d], self.s1x.at[d], self.r1x.at[d], self.here.xn))
        self.push(lambda: (self.mine(d, 3, self.low), self.f1y.at[d], self.s1y.at[d], self.r1y.at[d], self.here.yn))

    def sides(self, d):
        self.pair(1, d)
        self.landed(self.f1y.at[d], self.r1y.at[d])
        add_into(self.mine(d, 1, self.low), self.f1y.at[d])
        self.push(lambda: (self.mine(d, 1), self.f2x.at[d], self.s2x.at[d], self.r2x.at[d], self.here.xn))
        self.pair(2, d)
        if self.by_x:
            self.landed(self.f1x.at[d], self.r1x.at[d])
            add_into(self.mine(d, 2, self.top), self.f1x.at[d])
        self.push(lambda: (self.mine(d, 2), self.f2y.at[d], self.s2y.at[d], self.r2y.at[d], self.here.yn))

    def centre(self, d):
        self.pair(0, d)
        self.landed(self.f2x.at[d], self.r2x.at[d])
        self.landed(self.f2y.at[d], self.r2y.at[d])
        add_into(self.mine(d, 0), self.f2x.at[d], self.f2y.at[d])
        if d != 0:
            h = self.here
            self.push(lambda: (self.mine(d, 0), self.fz.at[h.z], self.sz.at[d], self.rz.at[h.z], h.at_z(h.zd(d))))

    def total(self):
        for d in (1, 2, 3):
            self.landed(self.fz.at[self.here.zd(d)], self.rz.at[self.here.zd(d)])
        b = self.block(0, 0, self.here.c)
        step = 32

        @pl.loop(0, 2 * self.rows // step)
        def _(i):
            n = i // (self.rows // step)
            r = pl.ds(pl.multiple_of((i % (self.rows // step)) * step, step), step)
            if self.whole:
                total = b[n, r, :].astype(F32)
                for d in (1, 2, 3):
                    total = total + self.fz[self.here.zd(d), n, r, :].astype(F32)
            else:
                total = jnp.where(self.here.z // 2 == n, b[0, r, :].astype(F32), 0.0)
                for d in (1, 2, 3):
                    total = total + jnp.where(self.here.zd(d) // 2 == n, self.fz[self.here.zd(d), 0, r, :].astype(F32), 0.0)
            self.tmp[n, r, :] = total.astype(self.tmp.dtype)

    def share(self, out):
        self.share_start()
        self.share_cross()
        self.share_end(out)

    def share_start(self):
        h = self.here
        self.keeps = [keep(self.tmp, self.full.at[h.t], self.osem.at[4])]
        self.push(lambda: (self.tmp, self.full.at[h.t], self.sg.at[0], self.rg.at[0], h.yn))
        self.push(lambda: (self.tmp, self.full.at[h.t], self.sg.at[1], self.rg.at[1], h.cn))

    def share_cross(self):
        h = self.here
        ty = 2 * (1 - h.y) + h.c
        self.landed(self.full.at[ty], self.rg.at[0])
        self.push(lambda: (self.full.at[ty], self.full.at[ty], self.sg.at[2], self.rg.at[2], h.cn))

    def share_end(self, out):
        h = self.here
        self.landed(self.full.at[2 * h.y + 1 - h.c], self.rg.at[1])
        self.landed(self.full.at[2 * (1 - h.y) + 1 - h.c], self.rg.at[2])
        self.keeps[0].wait()
        outs = [keep(self.full.at[q], out.at[:, :, pl.ds(q * self.cols, self.cols)], self.osem.at[q]) for q in range(4)]
        for copy in outs:
            copy.wait()

    def finish(self):
        for make in self.sends:
            remote(*make()).wait_send()
        for d in range(4):
            for e in range(2):
                for args in self.giving(d, e):
                    remote(*args).wait_send()


def wait_for(ref, sem, device):
    pltpu.make_async_remote_copy(
        src_ref=ref, dst_ref=ref, send_sem=sem, recv_sem=sem, device_id=device, device_id_type=MESH
    ).wait_recv()


def signed_tables(length, width):
    middle = width // 2
    frequency = rope_base ** (-np.arange(middle) * 2.0 / width)
    angles = np.arange(length)[:, None] * frequency[None, :]
    cosine, sine = np.cos(angles), np.sin(angles)
    return (
        jnp.asarray(np.concatenate([cosine, cosine], axis=1), F32),
        jnp.asarray(np.concatenate([-sine, sine], axis=1), F32),
    )


def dot_nn(a, b):
    return jnp.dot(a, b, preferred_element_type=F32)


def dot_nt(a, b):
    return lax.dot_general(a, b, (((1,), (1,)), ((), ())), preferred_element_type=F32)


def dot_tn(a, b):
    return lax.dot_general(a, b, (((0,), (0,)), ((), ())), preferred_element_type=F32)


BY_X = 64


class Weights:
    scratch = staticmethod(lambda: [pltpu.SemaphoreType.DMA((8, 4, 2))] * 4 + [pltpu.SemaphoreType.DMA((6,))])
    slots = 5

    def __init__(self, here, query, key, value, output, router, ids, w, wo, router_all, ids_all, sems):
        self.here = here
        self.query, self.output, self.w, self.wo = query, output, w, wo
        piece, part = query.shape[0], wo.shape[1]
        self.piece, self.part = piece, part
        hd = key.shape[1]
        self.shared = (
            (key, lambda f: w.at[span(f * piece, piece), pl.ds(part, hd)]),
            (value, lambda f: w.at[span(f * piece, piece), pl.ds(part + hd, hd)]),
            (router, lambda f: router_all.at[:, span(f * piece, piece)]),
            (ids, lambda f: ids_all.at[:, :, span(f * ids.shape[2], ids.shape[2])]),
        )
        self.qs, self.qr, self.ss, self.sr, self.loc = sems
        self.sends, self.keeps = [], []

    def landed(self, ref, sem):
        pltpu.make_async_remote_copy(
            src_ref=ref, dst_ref=ref, send_sem=sem, recv_sem=sem, device_id=self.here.xn, device_id_type=MESH
        ).wait_recv()

    def start_shared(self):
        h = self.here
        for n, (src, dst) in enumerate(self.shared):
            self.keeps.append(keep(src, dst(h.f), self.loc.at[n]))
            for d, e in ((2, 0), (1, 0), (3, 0), (0, 1)):
                self.sends.append(push(src, dst(h.f), self.ss.at[n, d, e], self.sr.at[n, (4 - d) % 4, e], h.peer(d, e)))

    def pass_shared(self, d):
        h = self.here
        for n, (_, dst) in enumerate(self.shared):
            ref = dst(2 * h.zr(d) + h.x)
            self.landed(ref, self.sr.at[n, d, 0])
            self.sends.append(push(ref, ref, self.ss.at[n, d, 1], self.sr.at[n, d, 1], h.xn))

    def wait_shared(self):
        h = self.here
        for n, (_, dst) in enumerate(self.shared):
            for d in range(4):
                self.landed(dst(2 * h.zr(d) + 1 - h.x), self.sr.at[n, d, 1])

    def start_pairs(self, n):
        h = self.here
        src, dst = ((self.query, self.w), (self.output, self.wo))[n]
        mine = lambda f: dst.at[span(f * self.piece, self.piece), pl.ds(0, self.part)]
        self.keeps.append(keep(src.at[:, span((h.f % 4) * self.part, self.part)], mine(h.f), self.loc.at[4 + n]))
        for d in (2, 1, 3, 0):
            for e in (1, 0):
                if d or e:
                    f = 2 * h.zr(d) + (h.x + e) % 2
                    self.sends.append(push(src.at[:, span((f % 4) * self.part, self.part)], mine(h.f),
                                           self.qs.at[n, d, e], self.qr.at[n, (4 - d) % 4, e], h.peer(d, e)))

    def wait_pairs(self, n, far=range(4)):
        h = self.here
        dst = (self.w, self.wo)[n]
        for d in far:
            for e in (1, 0):
                if d or e:
                    f = 2 * h.zr(d) + (h.x + e) % 2
                    self.landed(dst.at[span(f * self.piece, self.piece), pl.ds(0, self.part)], self.qr.at[n, d, e])

    def finish(self):
        for copy in self.sends:
            copy.wait_send()


def begin_kernel(heads, normed, cot, query, key, value, output, router, ids, cos_ref, sin_ref, qg_ref, kg_ref,
                 xn_out, w_out, wo_out, router_out, ids_out, cot_out, pre_out, qkv_out, prob_out, ctx_out, branch_out,
                 xn, w, wo, pre, qkv, prob, ctx, part, own, osem, *sems):
    here = Here()
    here.greet()
    at = 0
    x_rows = Gather(here, False, normed, xn, sems[at : at + Gather.slots], BY_X)
    at += Gather.slots
    c_rows = Gather(here, True, cot, cot_out, sems[at : at + Gather.slots], BY_X + 32, own)
    at += Gather.slots
    moved = Weights(here, query, key, value, output, router, ids, w, wo, router_out, ids_out, sems[at : at + Weights.slots])
    at += Weights.slots
    total = Sum(here, False, part, sems[at:], BY_X)

    x_rows.start()
    moved.start_shared()
    moved.start_pairs(0)
    x_rows.first_steps()
    for d in (1, 3, 2):
        moved.pass_shared(d)
    x_rows.last_steps()
    for d in (0,) + ORDER:
        x_rows.arrived(d, 0)
        x_rows.arrived(d, 1)
    moved.wait_shared()
    moved.wait_pairs(0, (2,))
    moved.start_pairs(1)
    moved.wait_pairs(0, (0, 1, 3))
    for copy in moved.keeps:
        copy.wait()
    outs = [keep(xn, xn_out, osem.at[0]), keep(w, w_out, osem.at[1])]

    seq = xn.shape[1]
    hd = cos_ref.shape[1]
    tile = 256
    scale = 1.0 / math.sqrt(hd)
    for i in range(seq // tile):
        r = pl.ds(i * tile, tile)
        got = dot_nn(xn[0, r, :], w[...])
        pre[r, :] = got[:, : (heads + 1) * hd]
        qkv[r, pl.ds((heads + 1) * hd, hd)] = got[:, (heads + 1) * hd :].astype(LOW)
        for a in range(heads + 1):
            one = got[:, a * hd : (a + 1) * hd]
            factor = lax.rsqrt(jnp.mean(one * one, axis=-1, keepdims=True) + norm_eps)
            gained = one * factor * (qg_ref if a < heads else kg_ref)[...]
            turned = gained * cos_ref[r, :] + pltpu.roll(gained, hd // 2, 1) * sin_ref[r, :]
            qkv[r, pl.ds(a * hd, hd)] = turned.astype(LOW)
    c_rows.start()
    outs += [keep(pre, pre_out, osem.at[2]), keep(qkv, qkv_out, osem.at[3])]
    for a in range(heads):
        for i in range(seq // tile):
            r = pl.ds(i * tile, tile)
            n = (i + 1) * tile
            score = dot_nt(qkv[r, pl.ds(a * hd, hd)], qkv[pl.ds(0, n), pl.ds(heads * hd, hd)]) * scale
            row = lax.broadcasted_iota(jnp.int32, (tile, n), 0) + i * tile
            col = lax.broadcasted_iota(jnp.int32, (tile, n), 1)
            score = jnp.where(col <= row, score, masked_score)
            terms = jnp.exp(score - jnp.max(score, axis=-1, keepdims=True))
            low = (terms * (1.0 / jnp.sum(terms, axis=-1, keepdims=True))).astype(LOW)
            prob[a, r, pl.ds(0, n)] = low
            ctx[r, pl.ds(a * hd, hd)] = dot_nn(low, qkv[pl.ds(0, n), pl.ds((heads + 1) * hd, hd)]).astype(LOW)
        if a == 0:
            c_rows.relay(1)
            c_rows.spread(1)
    outs += [keep(prob, prob_out, osem.at[4]), keep(ctx, ctx_out, osem.at[5])]
    moved.wait_pairs(1)
    outs.append(keep(wo, wo_out, osem.at[6]))
    rows = total.rows
    for e in (1, 0):
        for d in FAR_FIRST:
            at_f = span(here.number(d, e) * rows, rows)
            part[0, at_f, :] = dot_nt(ctx[at_f, :], wo[...]).astype(LOW)
            total.give(d, e)
    for d in FAR_FIRST:
        total.corner(d)
    c_rows.cross(0)
    c_rows.relay(2)
    c_rows.spread(2)
    for d in FAR_FIRST:
        total.sides(d)
    c_rows.cross(1)
    c_rows.relay(3)
    c_rows.spread(3)
    for d in FAR_FIRST:
        total.centre(d)
    c_rows.close(0)
    c_rows.cross(2)
    c_rows.close(1)
    total.total()
    total.share_start()
    c_rows.cross(3)
    c_rows.close(2)
    total.share_cross()
    c_rows.close(3)
    total.share_end(branch_out)
    for d in (0,) + ORDER:
        c_rows.arrived(d, 0)
        c_rows.arrived(d, 1)
    for each in (x_rows, c_rows, moved, total):
        each.finish()
    for copy in outs:
        copy.wait()


def begin(normed, cot, query, key, value, output, router, ids, cosine, sine, query_gain, key_gain):
    count, rows, width = normed.shape
    seq = rows * 8
    hd = query_gain.shape[0]
    part = query.shape[1] // 4
    heads = part // hd
    vm = pltpu.VMEM
    hbm = pl.BlockSpec(memory_space=pl.ANY)
    near = pl.BlockSpec(memory_space=pltpu.VMEM)
    shape = jax.ShapeDtypeStruct
    local = [
        ((1, seq, width), LOW),
        ((width, part + 2 * hd), LOW),
        ((width, part), LOW),
        ((seq, (heads + 1) * hd), F32),
        ((seq, (heads + 2) * hd), LOW),
        ((heads, seq, seq), LOW),
        ((seq, heads * hd), LOW),
    ]
    return pl.pallas_call(
        functools.partial(begin_kernel, heads),
        out_shape=(
            shape(*local[0]),
            shape(*local[1]),
            shape(*local[2]),
            shape((router.shape[0], width), LOW),
            shape((count, ids.shape[1], seq), jnp.int32),
            shape((count, seq, width), LOW),
            shape(*local[3]),
            shape(*local[4]),
            shape(*local[5]),
            shape(*local[6]),
            shape((count, rows, width), LOW),
        ),
        in_specs=[hbm] * 8 + [near] * 4,
        out_specs=[hbm] * 11,
        scratch_shapes=[vm(*entry) for entry in local]
        + [vm((1, seq, width), LOW), vm((count, rows, width), LOW), pltpu.SemaphoreType.DMA((7,))]
        + Gather.scratch() + Gather.scratch() + Weights.scratch() + Sum.scratch(1, rows, width, LOW, BY_X),
        compiler_params=pltpu.CompilerParams(
            collective_id=4, has_side_effects=True, vmem_limit_bytes=VMEM_LIMIT
        ),
        name="begin",
    )(normed, cot, query, key, value, output, router, ids, cosine, sine, query_gain[None], key_gain[None])


def experts_kernel(experts, expert_in, og_in, ids, router, g_in, u_in, d_in,
                   x_out, act_out, dx_sum, out_sum, probs_out, dgp_out,
                   x_t, g, u, dn, og_t, raw_s, act_t, dx, out, stage, share_s, dgp_t, dgp_got, dgp_all, dgp_c, dgp_y,
                   wsem, ogsem, xsem, actsem, psem, rsem, tsem, usem, *rest):
    here = Here()
    here.greet()
    by_x = expert_in.shape[1] // 2
    rows_x = Gather(here, True, expert_in, x_out, rest[: Gather.slots], by_x, x_t)
    sums = (
        Sum(here, True, dx, rest[Gather.slots : Gather.slots + Sum.slots], by_x),
        Sum(here, True, out, rest[Gather.slots + Sum.slots :], by_x),
    )
    number = here.number
    count, rows, width = expert_in.shape
    hidden = g.shape[0]
    per = hidden // experts
    tokens = count * rows
    lanes = router.shape[0]
    part = stage.shape[2]
    chunk = width // 4
    rows_x.start()
    loads = [keep(src, dst, wsem.at[n]) for n, (src, dst) in enumerate(((d_in, dn), (g_in, g), (u_in, u)))]

    def tile(i):
        return span(number(i // 2, i % 2) * rows, rows)

    def og_load(i):
        return pltpu.make_async_copy(og_in.at[:, tile(i), :], og_t.at[i % 2], ogsem.at[i % 2])

    def x_load(i):
        return pltpu.make_async_copy(x_out.at[:, tile(i), :], x_t, xsem.at[0])

    def act_store(i):
        return pltpu.make_async_copy(act_t.at[i % 2], act_out.at[:, :, tile(i), :], actsem.at[i % 2])

    def dgp_send(i):
        to = place(here.zd(i // 2), (here.x + i % 2) % 2, here.y, here.c)
        return remote(dgp_t.at[i], dgp_got.at[here.f], psem.at[i], rsem.at[here.f], to)

    def both(step, j):
        for each in sums:
            getattr(each, step)(j)

    early = {
        2: lambda: (rows_x.relay(1), rows_x.spread(1)),
        4: lambda: (rows_x.cross(0),),
        6: lambda: (rows_x.relay(2), rows_x.spread(2)),
        7: lambda: (rows_x.cross(1), rows_x.close(0)),
    }
    before = {
        1: lambda: (rows_x.relay(3), rows_x.spread(3), rows_x.arrived(0, 1)),
        2: lambda: (rows_x.arrived(1, 0), rows_x.arrived(1, 1)),
        3: lambda: (both("corner", 0),),
        4: lambda: (rows_x.arrived(2, 0), rows_x.arrived(2, 1)),
        5: lambda: (both("sides", 0), both("corner", 1)),
        6: lambda: (rows_x.arrived(3, 0), rows_x.arrived(3, 1)),
        7: lambda: (both("sides", 1), both("corner", 2), both("centre", 0)),
    }
    middle = {
        1: lambda: (rows_x.cross(2), rows_x.close(1)),
        2: lambda: (rows_x.cross(3), rows_x.close(2)),
        3: lambda: (rows_x.close(3),),
    }

    def hooks(table, i):
        for key, run in table.items():
            @pl.when(i == key)
            def _(run=run):
                run()

    row = lax.broadcasted_iota(jnp.int32, (lanes, hidden), 0)
    col = lax.broadcasted_iota(jnp.int32, (lanes, hidden), 1)
    spread = jnp.where(row == here.f * experts + col // per, 1.0, 0.0).astype(LOW)
    row8 = lax.broadcasted_iota(jnp.int32, (8, hidden), 0)
    col8 = lax.broadcasted_iota(jnp.int32, (8, hidden), 1)
    gather8 = jnp.where(row8 == col8 // per, 1.0, 0.0).astype(LOW)

    def first_half(i):
        x_tile = x_t[...].reshape(tokens, width)
        for n, right in enumerate((g, u)):
            for k in range(hidden // part):
                stage[n, pl.ds(k * tokens, tokens), :] = dot_nt(x_tile, right[pl.ds(k * part, part), :])
        logits = dot_nt(router[...], x_tile)
        named_ids = jnp.concatenate([ids[m, :, tile(i)] for m in range(count)], axis=1)
        lane = lax.broadcasted_iota(jnp.int32, logits.shape, 0)
        named = lane == named_ids[0:1, :]
        for k in range(1, named_ids.shape[0]):
            named = named | (lane == named_ids[k : k + 1, :])
        masked = jnp.where(named, logits, masked_score)
        terms = jnp.where(named, jnp.exp(masked - jnp.max(masked, axis=0, keepdims=True)), 0.0)
        probs = terms / jnp.sum(terms, axis=0, keepdims=True)
        high = probs.astype(LOW)
        low = (probs - high.astype(F32)).astype(LOW)
        share_s[...] = dot_tn(high, spread) + dot_tn(low, spread)
        return probs

    def between(i, m):
        r = pl.ds(m * rows, rows)
        gate, up = (
            jnp.concatenate([stage[n, pl.ds(k * tokens + m * rows, rows), :] for k in range(hidden // part)], axis=1)
            for n in range(2)
        )
        raw = raw_s[i, r, :].astype(F32)
        share = share_s[r, :]
        sig = 1.0 / (1.0 + jnp.exp(-gate))
        silu = gate * sig
        inner = silu * up
        product = inner * raw
        product_high = product.astype(LOW)
        product_low = (product - product_high.astype(F32)).astype(LOW)
        dgp_t[i, :, r] = dot_nt(gather8, product_high) + dot_nt(gather8, product_low)
        d_inner = raw * share
        act_t[i % 2, 0, m] = (d_inner * up * (sig + silu * (1.0 - sig))).astype(LOW)
        act_t[i % 2, 1, m] = (d_inner * silu).astype(LOW)
        act_t[i % 2, 2, m] = (inner * share).astype(LOW)

    def second_half(i, q):
        d_gate, d_up, weighted = (act_t[i % 2, n].reshape(tokens, hidden) for n in range(3))
        cols = pl.ds(q * chunk, chunk)
        got = dot_nn(d_gate, g[:, cols]) + dot_nn(d_up, u[:, cols])
        dx[:, tile(i), cols] = got.astype(LOW).reshape(count, rows, chunk)
        out[:, tile(i), cols] = dot_nn(weighted, dn[:, cols]).astype(LOW).reshape(count, rows, chunk)

    def sent(i):
        for each in sums:
            each.give(i // 2, i % 2)

        @pl.when(i > 0)
        def _():
            dgp_send(i).start()

    og_load(0).start()
    loads[0].wait()

    @pl.loop(0, 8)
    def _(i):
        @pl.when(i + 1 < 8)
        def _():
            og_load(i + 1).start()

        hooks(early, i)
        og_load(i).wait()
        raw_s[i] = dot_nt(og_t[i % 2].reshape(tokens, width), dn[...]).astype(LOW)

    loads[1].wait()
    loads[2].wait()
    rows_x.arrived(0, 0)
    probs_out[...] = first_half(0)
    for m in range(count):
        between(0, m)
    act_store(0).start()

    @pl.loop(1, 8)
    def _(i):
        hooks(before, i)
        x_load(i).start()

        @pl.when(i >= 2)
        def _():
            act_store(i - 2).wait()

        x_load(i).wait()
        first_half(i)
        hooks(middle, i)
        for m in range(count):
            second_half(i - 1, 2 * m)
            between(i, m)
            second_half(i - 1, 2 * m + 1)
        act_store(i).start()
        sent(i - 1)

    for q in range(4):
        second_half(7, q)
    sent(7)
    both("corner", 3)
    both("sides", 2)
    both("centre", 1)
    both("sides", 3)
    both("centre", 2)
    both("centre", 3)
    for d in range(4):
        for e in range(2):
            if d or e:
                n = number(d, e)
                wait_for(dgp_got.at[n], rsem.at[n], here.xn)
                dgp_all[n] = dgp_got[n]
    dgp_all[here.f] = dgp_t[0]
    first = push(dgp_all, dgp_c, tsem.at[0], usem.at[0], here.cn)
    sums[0].total()
    wait_for(dgp_c, usem.at[0], here.cn)
    first.wait_send()
    dgp_all[...] = dgp_all[...] + dgp_c[...]
    second = push(dgp_all, dgp_y, tsem.at[1], usem.at[1], here.yn)
    sums[0].share_start()
    sums[1].total()
    sums[1].share_start()
    sums[0].share_cross()
    sums[1].share_cross()
    sums[0].share_end(dx_sum)
    sums[1].share_end(out_sum)
    wait_for(dgp_y, usem.at[1], here.yn)
    dgp_out[...] = dgp_all[...] + dgp_y[...]
    second.wait_send()
    act_store(6).wait()
    act_store(7).wait()
    for i in range(1, 8):
        dgp_send(i).wait_send()
    rows_x.finish()
    for each in sums:
        each.finish()


def run_experts(expert_in, og, ids, router, gate, up, down):
    count, rows, width = expert_in.shape
    seq = rows * 8
    experts, per, _ = gate.shape
    hidden = experts * per
    tokens = count * rows
    lanes = router.shape[0]
    vm = pltpu.VMEM
    dma = pltpu.SemaphoreType.DMA
    hbm = pl.BlockSpec(memory_space=pl.ANY)
    near = pl.BlockSpec(memory_space=pltpu.VMEM)
    shape = jax.ShapeDtypeStruct
    total = Sum.scratch(count, rows, width, LOW, rows // 2)
    return pl.pallas_call(
        functools.partial(experts_kernel, experts),
        out_shape=(
            shape((count, seq, width), LOW),
            shape((3, count, seq, hidden), LOW),
            shape((count, rows, width), LOW),
            shape((count, rows, width), LOW),
            shape((lanes, tokens), F32),
            shape((8, 8, tokens), F32),
        ),
        in_specs=[hbm, hbm, near, near, hbm, hbm, hbm],
        out_specs=[hbm, hbm, hbm, hbm, near, near],
        scratch_shapes=[
            vm((count, rows, width), LOW),
            vm((hidden, width), LOW),
            vm((hidden, width), LOW),
            vm((hidden, width), LOW),
            vm((2, count, rows, width), LOW),
            vm((8, tokens, hidden), LOW),
            vm((2, 3, count, rows, hidden), LOW),
            vm((count, seq, width), LOW),
            vm((count, seq, width), LOW),
            vm((2, hidden // 256 * tokens, 256), F32),
            vm((tokens, hidden), F32),
            vm((8, 8, tokens), F32),
            vm((8, 8, tokens), F32),
            vm((8, 8, tokens), F32),
            vm((8, 8, tokens), F32),
            vm((8, 8, tokens), F32),
            dma((3,)),
            dma((2,)),
            dma((1,)),
            dma((2,)),
            dma((8,)),
            dma((8,)),
            dma((2,)),
            dma((2,)),
        ]
        + Gather.scratch()
        + total
        + total,
        compiler_params=pltpu.CompilerParams(
            collective_id=6, has_side_effects=True, vmem_limit_bytes=VMEM_LIMIT
        ),
        name="experts",
    )(expert_in, og, ids, router, gate.reshape(hidden, width), up.reshape(hidden, width), down.reshape(hidden, width))


def expert_grads_kernel(act, x, og, dg, du, dd):
    tokens = act.shape[1] * act.shape[2]
    x_cols = x[...].reshape(tokens, x.shape[2])
    og_cols = og[...].reshape(tokens, og.shape[2])
    for n, (right, out) in enumerate(((x_cols, dg), (x_cols, du), (og_cols, dd))):
        out[...] = dot_tn(act[n].reshape(tokens, act.shape[3]), right)


def expert_grads(act, x, og):
    _, count, seq, hidden = act.shape
    width = x.shape[2]
    block = min(512, width)
    cols = pl.BlockSpec((count, seq, block), lambda i: (0, 0, i))
    out = pl.BlockSpec((hidden, block), lambda i: (0, i))
    grads = jax.ShapeDtypeStruct((hidden, width), F32)
    return pl.pallas_call(
        expert_grads_kernel,
        grid=(width // block,),
        in_specs=[
            pl.BlockSpec(act.shape, lambda i: (0, 0, 0, 0), pipeline_mode=pl.Buffered(1)),
            cols,
            cols,
        ],
        out_specs=[out, out, out],
        out_shape=(grads, grads, grads),
        compiler_params=pltpu.CompilerParams(vmem_limit_bytes=VMEM_LIMIT),
        name="expert_grads",
    )(act, x, og)


PEERS = tuple((d, e) for d in (2, 1, 3, 0) for e in (1, 0) if d or e)


def end_kernel(heads, d_branch, xn_in, w_in, wo_in, pre_in, qkv_in, prob_in, ctx_in, aux, query, key, value,
               cos_ref, sin_ref, qg_ref, kg_ref,
               dn_sum, dq_out, dk_out, dv_out, do_out, aux_out, gains_out,
               db, xn, w, wo, pre, qkv, prob, ctx, dctx, dq_s, dk_s, dv_s, dqkv, dwo, dw, dwo_got, dwq_got, kv_x, kv_z,
               aux_got, head_part, head_got, line, line_c, line_y, wide_q, wide_o, wide_kv,
               lsem, psem, rsem, kxs, kxr, kzs, kzr, tsem, usem, osem, *rest):
    here = Here()
    here.greet()
    sends, outs = [], []
    rows_db = Gather(here, False, d_branch, db, rest[: Gather.slots], BY_X)
    at = Gather.slots
    dn = Sum(here, False, db, rest[at:], BY_X)
    rows = dn.rows
    piece, part = query.shape[0], wo.shape[1]
    seq = xn.shape[1]
    hd = cos_ref.shape[1]
    tile = 256
    scale = 1.0 / math.sqrt(hd)

    def number(d, e):
        return 2 * here.zr(d) + (here.x + e) % 2

    def send(n, d, e, src, got):
        sends.append(push(src, got.at[(4 - d) % 4, e], psem.at[n, d, e], rsem.at[n, (4 - d) % 4, e], here.peer(d, e)))

    def got_from(n, d, e, got):
        wait_for(got.at[d, e], rsem.at[n, d, e], here.xn)
        return got[d, e]

    rows_db.start()
    loads = {}
    for n, (src, dst) in enumerate(((wo_in, wo), (ctx_in, ctx), (qkv_in, qkv), (prob_in, prob), (pre_in, pre),
                                    (xn_in, xn), (w_in, w))):
        loads[n] = keep(src, dst, lsem.at[n])
    for d, e in PEERS:
        send(0, d, e, aux.at[number(d, e)], aux_got)
    rows_db.first_steps()
    rows_db.last_steps()
    for d in (0,) + ORDER:
        rows_db.arrived(d, 0)
        rows_db.arrived(d, 1)
    for n in range(7):
        loads[n].wait()

    for i in range(seq // tile):
        r = pl.ds(i * tile, tile)
        dctx[r, :] = dot_nn(db[0, r, :], wo[...]).astype(LOW)
    for d, e in PEERS + ((0, 0),):
        r = span(number(d, e) * piece, piece)
        dwo[r, :] = dot_tn(db[0, :, r], ctx[...]).astype(LOW)
        if d or e:
            send(1, d, e, dwo.at[r, :], dwo_got)
    dk_s[...] = jnp.zeros_like(dk_s)
    dv_s[...] = jnp.zeros_like(dv_s)
    for a in range(heads):
        for i in range(seq // tile):
            r = pl.ds(i * tile, tile)
            n = (i + 1) * tile
            q_tile = qkv[r, pl.ds(a * hd, hd)]
            k_rows = qkv[pl.ds(0, n), pl.ds(heads * hd, hd)]
            v_rows = qkv[pl.ds(0, n), pl.ds((heads + 1) * hd, hd)]
            up = dctx[r, pl.ds(a * hd, hd)]
            low = prob[a, r, pl.ds(0, n)]
            wide = low.astype(F32)
            dprob = dot_nt(up, v_rows)
            delta = jnp.sum(wide * dprob, axis=-1, keepdims=True)
            dscore = (wide * (dprob - delta)).astype(LOW)
            dq_s[r, pl.ds(a * hd, hd)] = dot_nn(dscore, k_rows) * scale
            dk_s[pl.ds(0, n), :] += dot_tn(dscore, q_tile) * scale
            dv_s[pl.ds(0, n), :] += dot_tn(low, up)
    gq = jnp.zeros((1, hd), F32)
    gk = jnp.zeros((1, hd), F32)
    for i in range(seq // tile):
        r = pl.ds(i * tile, tile)
        dqkv[r, pl.ds((heads + 1) * hd, hd)] = dv_s[r, :].astype(LOW)
        for a in range(heads + 1):
            up = dq_s[r, pl.ds(a * hd, hd)] if a < heads else dk_s[r, :]
            one = pre[r, pl.ds(a * hd, hd)]
            factor = lax.rsqrt(jnp.mean(one * one, axis=-1, keepdims=True) + norm_eps)
            hat = one * factor
            turned = up * cos_ref[r, :] + pltpu.roll(up * sin_ref[r, :], hd // 2, 1)
            gain_part = jnp.sum(turned * hat, axis=0, keepdims=True)
            gained = turned * (qg_ref if a < heads else kg_ref)[...]
            back = factor * (gained - hat * jnp.mean(gained * hat, axis=-1, keepdims=True))
            dqkv[r, pl.ds(a * hd, hd)] = back.astype(LOW)
            if a < heads:
                gq = gq + gain_part
            else:
                gk = gk + gain_part
    head_part[...] = jnp.concatenate([gq, gk, jnp.zeros((6, hd), F32)], axis=0)
    for d, e in PEERS:
        send(3, d, e, head_part, head_got)
    rows_db.finish()
    for e in (1, 0):
        for d in FAR_FIRST:
            r = span(here.number(d, e) * rows, rows)
            db[0, r, :] = dot_nt(dqkv[r, :], w[...]).astype(LOW)
            dn.give(d, e)
    for d, e in PEERS + ((0, 0),):
        r = span(number(d, e) * piece, piece)
        dw[r, :] = dot_tn(xn[0, :, r], dqkv[...]).astype(LOW)
        if d or e:
            send(2, d, e, dw.at[r, pl.ds(0, part)], dwq_got)
        if e:
            sends.append(push(dw.at[r, pl.ds(part, 2 * hd)], kv_x.at[d], kxs.at[d], kxr.at[d], here.xn))
    for d in FAR_FIRST:
        dn.corner(d)
    for d in (2, 1, 3, 0):
        r = span(number(d, 0) * piece, piece)
        wait_for(kv_x.at[d], kxr.at[d], here.xn)
        both = dw[r, pl.ds(part, 2 * hd)].astype(F32) + kv_x[d].astype(F32)
        dw[r, pl.ds(part, 2 * hd)] = both.astype(LOW)
        if d:
            there = (4 - d) % 4
            sends.append(push(dw.at[r, pl.ds(part, 2 * hd)], kv_z.at[there], kzs.at[d], kzr.at[there], here.peer(d, 0)))
    for d in FAR_FIRST:
        dn.sides(d)
    for d in FAR_FIRST:
        dn.centre(d)

    def merged(n, wide, got, mine):
        for d in (0, 1):
            for e in (0, 1):
                first = mine if (d, e) == (0, 0) else got_from(n, d, e, got)
                both = first.astype(F32) + got_from(n, d + 2, e, got).astype(F32)
                wide[:, span((number(d, e) % 4) * part, part)] = both

    own = span(here.f * piece, piece)
    merged(1, wide_o, dwo_got, dwo[own, :])
    outs.append(keep(wide_o, do_out, osem.at[0]))
    aux_total = aux[here.f].astype(F32)
    for d, e in PEERS:
        aux_total = aux_total + got_from(0, d, e, aux_got).astype(F32)
    aux_out[...] = aux_total
    head_total = head_part[...]
    for d, e in PEERS:
        head_total = head_total + got_from(3, d, e, head_got)
    line[:, pl.ds(piece, hd)] = head_total
    dn.total()
    dn.share(dn_sum)
    merged(2, wide_q, dwq_got, dw[own, pl.ds(0, part)])
    outs.append(keep(wide_q, dq_out, osem.at[1]))
    kv = dw[own, pl.ds(part, 2 * hd)].astype(F32)
    for d in (1, 2, 3):
        wait_for(kv_z.at[d], kzr.at[d], here.xn)
        kv = kv + kv_z[d].astype(F32)
    wide_kv[...] = kv
    outs.append(keep(wide_kv.at[:, pl.ds(0, hd)], dk_out, osem.at[2]))
    outs.append(keep(wide_kv.at[:, pl.ds(hd, hd)], dv_out, osem.at[3]))

    def row_sums(product):
        high = product.astype(LOW)
        rest_ = (product - high.astype(F32)).astype(LOW)
        ones = jnp.ones((8, product.shape[1]), LOW)
        return dot_nt(ones, high) + dot_nt(ones, rest_)

    line[:, pl.ds(0, piece)] = (
        row_sums(query[...].astype(F32) * wide_q[...])
        + row_sums(key[...].astype(F32) * kv[:, :hd])
        + row_sums(value[...].astype(F32) * kv[:, hd:])
    )
    first = push(line, line_c, tsem.at[0], usem.at[0], here.cn)
    wait_for(line_c, usem.at[0], here.cn)
    first.wait_send()
    line[...] = line[...] + line_c[...]
    second = push(line, line_y, tsem.at[1], usem.at[1], here.yn)
    wait_for(line_y, usem.at[1], here.yn)
    gains_out[...] = line[...] + line_y[...]
    second.wait_send()
    dn.finish()
    for copy in sends:
        copy.wait_send()
    for copy in outs:
        copy.wait()


def end(d_branch, xn, w, wo, pre, qkv, prob, ctx, aux, query, key, value, cosine, sine, query_gain, key_gain):
    count, rows, width = d_branch.shape
    seq = rows * 8
    hd = query_gain.shape[0]
    piece, local = query.shape
    part = local // 4
    heads = part // hd
    vm = pltpu.VMEM
    dma = pltpu.SemaphoreType.DMA
    hbm = pl.BlockSpec(memory_space=pl.ANY)
    near = pl.BlockSpec(memory_space=pltpu.VMEM)
    shape = jax.ShapeDtypeStruct
    return pl.pallas_call(
        functools.partial(end_kernel, heads),
        out_shape=(
            shape((count, rows, width), LOW),
            shape((piece, local), F32),
            shape((piece, hd), F32),
            shape((piece, hd), F32),
            shape((piece, local), F32),
            shape(aux.shape[1:], F32),
            shape((8, piece + hd), F32),
        ),
        in_specs=[hbm] * 8 + [near] * 8,
        out_specs=[hbm] * 5 + [near] * 2,
        scratch_shapes=[
            vm((1, seq, width), LOW),
            vm((1, seq, width), LOW),
            vm(w.shape, LOW),
            vm(wo.shape, LOW),
            vm(pre.shape, F32),
            vm(qkv.shape, LOW),
            vm(prob.shape, LOW),
            vm(ctx.shape, LOW),
            vm(ctx.shape, LOW),
            vm((seq, heads * hd), F32),
            vm((seq, hd), F32),
            vm((seq, hd), F32),
            vm((seq, (heads + 2) * hd), LOW),
            vm((width, part), LOW),
            vm((width, part + 2 * hd), LOW),
            vm((4, 2, piece, part), LOW),
            vm((4, 2, piece, part), LOW),
            vm((4, piece, 2 * hd), LOW),
            vm((4, piece, 2 * hd), LOW),
            vm((4, 2) + aux.shape[1:], LOW),
            vm((8, hd), F32),
            vm((4, 2, 8, hd), F32),
            vm((8, piece + hd), F32),
            vm((8, piece + hd), F32),
            vm((8, piece + hd), F32),
            vm((piece, local), F32),
            vm((piece, local), F32),
            vm((piece, 2 * hd), F32),
            dma((7,)),
            dma((4, 4, 2)),
            dma((4, 4, 2)),
            dma((4,)),
            dma((4,)),
            dma((4,)),
            dma((4,)),
            dma((2,)),
            dma((2,)),
            dma((4,)),
        ]
        + Gather.scratch()
        + Sum.scratch(1, rows, width, LOW, BY_X),
        compiler_params=pltpu.CompilerParams(
            collective_id=5, has_side_effects=True, vmem_limit_bytes=VMEM_LIMIT
        ),
        name="end",
    )(d_branch, xn, w, wo, pre, qkv, prob, ctx, aux, query, key, value, cosine, sine,
      query_gain[None], key_gain[None])


def rotate_half(values):
    middle = values.shape[-1] // 2
    return jnp.concatenate([-values[..., middle:], values[..., :middle]], axis=-1)


def rope_tables(positions, head_width):
    middle = head_width // 2
    frequency = rope_base ** (-jnp.arange(middle, dtype=jnp.float32) * 2.0 / head_width)
    angles = positions.astype(jnp.float32)[:, None] * frequency[None, :]
    angles = jnp.concatenate([angles, angles], axis=1)
    return (jnp.cos(angles), jnp.sin(angles))


def norm_parts(values):
    factor = lax.rsqrt(jnp.mean(values * values, axis=-1, keepdims=True) + norm_eps)
    return (values * factor, factor)


def norm_back(upstream, gain, normal, factor):
    scaled = upstream * gain
    return factor * (scaled - normal * jnp.mean(scaled * normal, axis=-1, keepdims=True))


def head_back(upstream, cosine_heads, sine_heads, gain, normal, factor):
    turned = upstream * cosine_heads - rotate_half(upstream * sine_heads)
    gain_part = jnp.sum(turned * normal, axis=(0, 1))
    return (norm_back(turned, gain, normal, factor), gain_part)


def fetch_weights(query_weight, key_weight, value_weight, output_weight, router_weight):
    return (
        lax.all_gather(query_weight, "fsdp", axis=0, tiled=True),
        lax.all_gather(key_weight, "fsdp", axis=0, tiled=True),
        lax.all_gather(value_weight, "fsdp", axis=0, tiled=True),
        lax.all_gather(output_weight, "fsdp", axis=0, tiled=True),
        lax.all_gather(router_weight, "fsdp", axis=0, tiled=True),
    )


def widen(summed):
    return lax.all_gather(summed, "tp", axis=3, tiled=True)


def carry_back(summed):
    return lax.all_to_all(summed, "fsdp", split_axis=0, concat_axis=0, tiled=True)


def send_home(summed):
    arrived_home = carry_back(widen(summed))
    return arrived_home


def general_device(
    tokens,
    cotangent,
    expert_ids,
    attention_gain,
    query_gain,
    key_gain,
    query_weight,
    key_weight,
    value_weight,
    output_weight,
    expert_gain,
    router_weight,
    gate_weight,
    up_weight,
    down_weight,
):
    micro_count = tokens.shape[0]
    tok_rows = tokens.shape[1]
    width = tokens.shape[2]
    route_count = expert_ids.shape[2]
    head_dim = query_gain.shape[0]
    local_heads = query_weight.shape[1] // head_dim
    local_groups = key_weight.shape[1] // head_dim
    group_size = local_heads // local_groups
    fsdp_count = lax.axis_size("fsdp")
    seq_len = tok_rows * fsdp_count
    experts_here = gate_weight.shape[0]
    expert_count = experts_here * fsdp_count
    capacity = max(2, 5 * tok_rows * route_count // (4 * expert_count))
    key_block = math.gcd(seq_len, 512)
    score_scale = 1.0 / math.sqrt(head_dim)
    query_count = tok_rows * group_size
    routed_total = tok_rows * route_count
    start_row = lax.axis_index("fsdp") * tok_rows
    positions = start_row + jnp.arange(tok_rows, dtype=jnp.int32)
    cosine_table, sine_table = rope_tables(positions, head_dim)
    cosine_heads = cosine_table[:, None, :]
    sine_heads = sine_table[:, None, :]
    query_pos = start_row + jnp.arange(query_count, dtype=jnp.int32) // group_size
    block_total = (start_row + tok_rows + key_block - 1) // key_block
    expert_range = jnp.arange(expert_count, dtype=jnp.int32)
    zero_row = jnp.zeros((1, width), jnp.bfloat16)

    def to_rows(tensor):
        return (
            tensor.reshape(tok_rows, local_groups, group_size, head_dim)
            .transpose(1, 0, 2, 3)
            .reshape(local_groups, query_count, head_dim)
        )

    def from_rows(tensor):
        return (
            tensor.reshape(local_groups, tok_rows, group_size, head_dim)
            .transpose(1, 0, 2, 3)
            .reshape(tok_rows, local_heads, head_dim)
        )

    acc_attention_gain = jnp.zeros((width,), jnp.float32)
    acc_head_gains = jnp.zeros((2, head_dim), jnp.float32)
    acc_query = jnp.zeros((width, local_heads * head_dim), jnp.float32)
    acc_key = jnp.zeros((width, local_groups * head_dim), jnp.float32)
    acc_value = jnp.zeros((width, local_groups * head_dim), jnp.float32)
    acc_output = jnp.zeros((width, local_heads * head_dim), jnp.float32)
    acc_expert_gain = jnp.zeros((width,), jnp.float32)
    acc_router = jnp.zeros((width, expert_count), jnp.float32)
    acc_gate = jnp.zeros(gate_weight.shape, jnp.float32)
    acc_up = jnp.zeros(up_weight.shape, jnp.float32)
    acc_down = jnp.zeros(down_weight.shape, jnp.float32)
    layer_rows = []
    input_rows = []
    for micro_index in range(micro_count):
        inputs = tokens[micro_index].astype(jnp.float32)
        query_full, key_full, value_full, output_full, router_full = fetch_weights(
            query_weight, key_weight, value_weight, output_weight, router_weight
        )
        input_hat, attention_factor = norm_parts(inputs)
        normed = (input_hat * attention_gain).astype(jnp.bfloat16)
        query_pre = jnp.dot(normed, query_full, preferred_element_type=jnp.float32).reshape(
            tok_rows, local_heads, head_dim
        )
        key_pre = jnp.dot(normed, key_full, preferred_element_type=jnp.float32).reshape(
            tok_rows, local_groups, head_dim
        )
        value_low = jnp.dot(normed, value_full, preferred_element_type=jnp.float32).astype(
            jnp.bfloat16
        )
        query_hat, query_factor = norm_parts(query_pre)
        key_hat, key_factor = norm_parts(key_pre)
        query_scaled = query_hat * query_gain
        key_scaled = key_hat * key_gain
        query_low = (query_scaled * cosine_heads + rotate_half(query_scaled) * sine_heads).astype(
            jnp.bfloat16
        )
        key_low = (key_scaled * cosine_heads + rotate_half(key_scaled) * sine_heads).astype(
            jnp.bfloat16
        )
        key_all, value_all = (
            lax.all_gather(
                key_low.reshape(tok_rows, local_groups * head_dim), "fsdp", axis=0, tiled=True
            ),
            lax.all_gather(value_low, "fsdp", axis=0, tiled=True),
        )
        key_heads = key_all.reshape(seq_len, local_groups, head_dim).transpose(1, 0, 2)
        value_heads = value_all.reshape(seq_len, local_groups, head_dim).transpose(1, 0, 2)
        query_rows = to_rows(query_low)

        def scores_at(block_index):
            block_start = block_index * key_block
            key_slice = lax.dynamic_slice_in_dim(key_heads, block_start, key_block, 1)
            raw_scores = (
                jnp.einsum(
                    "gqd,gkd->gqk", query_rows, key_slice, preferred_element_type=jnp.float32
                )
                * score_scale
            )
            allowed = (block_start + jnp.arange(key_block, dtype=jnp.int32))[None, :] <= query_pos[
                :, None
            ]
            return (jnp.where(allowed[None], raw_scores, masked_score), allowed, block_start)

        def stats_step(block_index, carried):
            run_peak, run_total = carried
            scores, allowed, block_start = scores_at(block_index)
            new_peak = jnp.maximum(run_peak, jnp.max(scores, axis=-1))
            terms = jnp.where(allowed[None], jnp.exp(scores - new_peak[..., None]), 0.0)
            return (new_peak, run_total * jnp.exp(run_peak - new_peak) + jnp.sum(terms, axis=-1))

        start_stats = (
            jnp.full((local_groups, query_count), masked_score, jnp.float32),
            jnp.zeros((local_groups, query_count), jnp.float32),
        )
        run_peak, run_total = lax.fori_loop(0, block_total, stats_step, start_stats)
        log_total = run_peak + jnp.log(run_total)

        def value_step(block_index, acc_context):
            scores, allowed, block_start = scores_at(block_index)
            probs_low = jnp.where(
                allowed[None], jnp.exp(scores - log_total[..., None]), 0.0
            ).astype(jnp.bfloat16)
            value_slice = lax.dynamic_slice_in_dim(value_heads, block_start, key_block, 1)
            return acc_context + jnp.einsum(
                "gqk,gkd->gqd", probs_low, value_slice, preferred_element_type=jnp.float32
            )

        context_rows = lax.fori_loop(
            0,
            block_total,
            value_step,
            jnp.zeros((local_groups, query_count, head_dim), jnp.float32),
        )
        context_low = (
            from_rows(context_rows).reshape(tok_rows, local_heads * head_dim).astype(jnp.bfloat16)
        )
        branch_part = jnp.einsum(
            "th,dh->td", context_low, output_full, preferred_element_type=jnp.float32
        )
        resid = inputs + lax.psum(branch_part.astype(jnp.bfloat16), "tp").astype(jnp.float32)
        resid_hat, expert_factor = norm_parts(resid)
        expert_in = (resid_hat * expert_gain).astype(jnp.bfloat16)
        logits = jnp.dot(expert_in, router_full, preferred_element_type=jnp.float32)
        routes_now = expert_ids[micro_index]
        choose = (routes_now[:, :, None] == expert_range[None, None, :]).astype(jnp.float32)
        picked = jnp.sum(choose * logits[:, None, :], axis=-1)
        shifted = jnp.exp(picked - jnp.max(picked, axis=-1, keepdims=True))
        gate_probs = shifted / jnp.sum(shifted, axis=-1, keepdims=True)
        flat_routes = routes_now.reshape(-1)
        onehot = (flat_routes[:, None] == expert_range[None, :]).astype(jnp.int32)
        rank_in = jnp.sum((jnp.cumsum(onehot, axis=0) - onehot) * onehot, axis=1)
        slot_index = flat_routes * capacity + rank_in
        slot_source = (
            jnp.full((expert_count * capacity,), routed_total, jnp.int32)
            .at[slot_index]
            .set(jnp.arange(routed_total, dtype=jnp.int32))
        )
        padded_in = jnp.concatenate([expert_in, zero_row], axis=0)
        outgoing = padded_in[slot_source // route_count].reshape(
            fsdp_count, experts_here, capacity, width
        )
        arrived = lax.all_to_all(outgoing, "fsdp", split_axis=0, concat_axis=0, tiled=True)
        gate_pre = jnp.einsum(
            "secd,efd->secf", arrived, gate_weight, preferred_element_type=jnp.float32
        )
        up_pre = jnp.einsum(
            "secd,efd->secf", arrived, up_weight, preferred_element_type=jnp.float32
        )
        gate_sigmoid = jax.nn.sigmoid(gate_pre)
        inner_low = (gate_pre * gate_sigmoid * up_pre).astype(jnp.bfloat16)
        result_part = jnp.einsum(
            "secf,efd->secd", inner_low, down_weight, preferred_element_type=jnp.float32
        )
        result_low = lax.psum_scatter(
            result_part.astype(jnp.bfloat16), "tp", scatter_dimension=3, tiled=True
        )
        result_home = send_home(result_low)
        routed = (
            result_home.reshape(expert_count * capacity, width)[slot_index]
            .astype(jnp.float32)
            .reshape(tok_rows, route_count, width)
        )
        layer_rows.append(
            (resid + jnp.sum(gate_probs[:, :, None] * routed, axis=1)).astype(jnp.bfloat16)
        )
        query_full, key_full, value_full, output_full, router_full = fetch_weights(
            query_weight, key_weight, value_weight, output_weight, router_weight
        )
        out_grad = cotangent[micro_index].astype(jnp.float32)
        d_route = (
            (gate_probs[:, :, None] * out_grad[:, None, :])
            .astype(jnp.bfloat16)
            .reshape(routed_total, width)
        )
        d_gate_probs = jnp.sum(out_grad[:, None, :] * routed, axis=-1)
        d_pick = gate_probs * (
            d_gate_probs - jnp.sum(gate_probs * d_gate_probs, axis=-1, keepdims=True)
        )
        d_logits = jnp.sum(choose * d_pick[:, :, None], axis=1).astype(jnp.bfloat16)
        grad_outgoing = jnp.concatenate([d_route, zero_row], axis=0)[slot_source].reshape(
            fsdp_count, experts_here, capacity, width
        )
        grad_arrived = lax.all_to_all(
            grad_outgoing, "fsdp", split_axis=0, concat_axis=0, tiled=True
        )
        d_inner = jnp.einsum(
            "secd,efd->secf", grad_arrived, down_weight, preferred_element_type=jnp.float32
        )
        acc_down = acc_down + jnp.einsum(
            "secf,secd->efd", inner_low, grad_arrived, preferred_element_type=jnp.float32
        )
        d_gate_low = (
            d_inner * up_pre * gate_sigmoid * (1.0 + gate_pre * (1.0 - gate_sigmoid))
        ).astype(jnp.bfloat16)
        d_up_low = (d_inner * gate_pre * gate_sigmoid).astype(jnp.bfloat16)
        acc_gate = acc_gate + jnp.einsum(
            "secf,secd->efd", d_gate_low, arrived, preferred_element_type=jnp.float32
        )
        acc_up = acc_up + jnp.einsum(
            "secf,secd->efd", d_up_low, arrived, preferred_element_type=jnp.float32
        )
        d_copy_part = jnp.einsum(
            "secf,efd->secd", d_gate_low, gate_weight, preferred_element_type=jnp.float32
        ) + jnp.einsum("secf,efd->secd", d_up_low, up_weight, preferred_element_type=jnp.float32)
        d_copy_low = lax.psum_scatter(
            d_copy_part.astype(jnp.bfloat16), "tp", scatter_dimension=3, tiled=True
        )
        d_copy_home = send_home(d_copy_low)
        d_copies = (
            d_copy_home.reshape(expert_count * capacity, width)[slot_index]
            .astype(jnp.float32)
            .reshape(tok_rows, route_count, width)
        )
        d_expert_in = jnp.sum(d_copies, axis=1) + jnp.dot(
            d_logits, router_full.T, preferred_element_type=jnp.float32
        )
        acc_router = acc_router + jnp.dot(expert_in.T, d_logits, preferred_element_type=jnp.float32)
        acc_expert_gain = acc_expert_gain + jnp.sum(d_expert_in * resid_hat, axis=0)
        d_resid = out_grad + norm_back(d_expert_in, expert_gain, resid_hat, expert_factor)
        d_branch = d_resid.astype(jnp.bfloat16)
        acc_output = acc_output + jnp.einsum(
            "td,th->dh", d_branch, context_low, preferred_element_type=jnp.float32
        )
        d_context = jnp.dot(d_branch, output_full, preferred_element_type=jnp.float32).astype(
            jnp.bfloat16
        )
        d_context_rows = to_rows(d_context.reshape(tok_rows, local_heads, head_dim))
        delta_rows = jnp.sum(d_context_rows.astype(jnp.float32) * context_rows, axis=-1)

        def grad_step(block_index, carried):
            d_query_rows, key_grads_all = carried
            scores, allowed, block_start = scores_at(block_index)
            probs = jnp.where(allowed[None], jnp.exp(scores - log_total[..., None]), 0.0)
            key_slice = lax.dynamic_slice_in_dim(key_heads, block_start, key_block, 1)
            value_slice = lax.dynamic_slice_in_dim(value_heads, block_start, key_block, 1)
            d_probs = jnp.einsum(
                "gqd,gkd->gqk", d_context_rows, value_slice, preferred_element_type=jnp.float32
            )
            d_scores = (probs * (d_probs - delta_rows[..., None])).astype(jnp.bfloat16)
            d_query_rows = (
                d_query_rows
                + jnp.einsum(
                    "gqk,gkd->gqd", d_scores, key_slice, preferred_element_type=jnp.float32
                )
                * score_scale
            )
            d_key_block = (
                jnp.einsum("gqk,gqd->kgd", d_scores, query_rows, preferred_element_type=jnp.float32)
                * score_scale
            )
            d_value_block = jnp.einsum(
                "gqk,gqd->kgd",
                probs.astype(jnp.bfloat16),
                d_context_rows,
                preferred_element_type=jnp.float32,
            )
            current = lax.dynamic_slice_in_dim(key_grads_all, block_start, key_block, 0)
            updated = current + jnp.concatenate([d_key_block, d_value_block], axis=-1)
            return (
                d_query_rows,
                lax.dynamic_update_slice_in_dim(key_grads_all, updated, block_start, 0),
            )

        start_grads = (
            jnp.zeros((local_groups, query_count, head_dim), jnp.float32),
            jnp.zeros((seq_len, local_groups, 2 * head_dim), jnp.float32),
        )
        d_query_rows, key_grads_all = lax.fori_loop(0, block_total, grad_step, start_grads)
        key_grads = (
            lax.psum_scatter(
                key_grads_all.reshape(seq_len, local_groups * 2 * head_dim).astype(jnp.bfloat16),
                "fsdp",
                scatter_dimension=0,
                tiled=True,
            )
            .astype(jnp.float32)
            .reshape(tok_rows, local_groups, 2 * head_dim)
        )
        d_value_low = (
            key_grads[..., head_dim:]
            .reshape(tok_rows, local_groups * head_dim)
            .astype(jnp.bfloat16)
        )
        d_key_pre, key_gain_part = head_back(
            key_grads[..., :head_dim], cosine_heads, sine_heads, key_gain, key_hat, key_factor
        )
        d_query_pre, query_gain_part = head_back(
            from_rows(d_query_rows), cosine_heads, sine_heads, query_gain, query_hat, query_factor
        )
        d_query_low = d_query_pre.astype(jnp.bfloat16).reshape(tok_rows, local_heads * head_dim)
        d_key_low = d_key_pre.astype(jnp.bfloat16).reshape(tok_rows, local_groups * head_dim)
        d_normed_part = jnp.dot(d_query_low, query_full.T, preferred_element_type=jnp.float32)
        d_normed_part = d_normed_part + jnp.dot(
            d_key_low, key_full.T, preferred_element_type=jnp.float32
        )
        d_normed_part = d_normed_part + jnp.dot(
            d_value_low, value_full.T, preferred_element_type=jnp.float32
        )
        acc_query = acc_query + jnp.dot(normed.T, d_query_low, preferred_element_type=jnp.float32)
        acc_key = acc_key + jnp.dot(normed.T, d_key_low, preferred_element_type=jnp.float32)
        acc_value = acc_value + jnp.dot(normed.T, d_value_low, preferred_element_type=jnp.float32)
        d_normed, head_gain_parts = (
            lax.psum(d_normed_part.astype(jnp.bfloat16), "tp").astype(jnp.float32),
            lax.psum(jnp.stack([query_gain_part, key_gain_part]).astype(jnp.bfloat16), "tp").astype(
                jnp.float32
            ),
        )
        acc_head_gains = acc_head_gains + head_gain_parts
        acc_attention_gain = acc_attention_gain + jnp.sum(d_normed * input_hat, axis=0)
        input_rows.append(
            (d_resid + norm_back(d_normed, attention_gain, input_hat, attention_factor)).astype(
                jnp.bfloat16
            )
        )
    summed = (
        lax.psum_scatter(
            acc_attention_gain.astype(jnp.bfloat16), "fsdp", scatter_dimension=0, tiled=True
        ).astype(jnp.float32),
        lax.psum_scatter(
            acc_head_gains[0].astype(jnp.bfloat16), "fsdp", scatter_dimension=0, tiled=True
        ).astype(jnp.float32),
        lax.psum_scatter(
            acc_head_gains[1].astype(jnp.bfloat16), "fsdp", scatter_dimension=0, tiled=True
        ).astype(jnp.float32),
        lax.psum_scatter(
            acc_query.astype(jnp.bfloat16), "fsdp", scatter_dimension=0, tiled=True
        ).astype(jnp.float32),
        lax.psum_scatter(
            acc_key.astype(jnp.bfloat16), "fsdp", scatter_dimension=0, tiled=True
        ).astype(jnp.float32),
        lax.psum_scatter(
            acc_value.astype(jnp.bfloat16), "fsdp", scatter_dimension=0, tiled=True
        ).astype(jnp.float32),
        lax.psum_scatter(
            acc_output.astype(jnp.bfloat16), "fsdp", scatter_dimension=0, tiled=True
        ).astype(jnp.float32),
        lax.psum_scatter(
            acc_expert_gain.astype(jnp.bfloat16), "fsdp", scatter_dimension=0, tiled=True
        ).astype(jnp.float32),
        lax.psum_scatter(
            acc_router.astype(jnp.bfloat16), "fsdp", scatter_dimension=0, tiled=True
        ).astype(jnp.float32),
    )
    return (
        jnp.stack(layer_rows),
        jnp.stack(input_rows),
        summed[0],
        summed[1],
        summed[2],
        summed[3],
        summed[4],
        summed[5],
        summed[6],
        summed[7],
        summed[8],
        acc_gate,
        acc_up,
        acc_down,
    )


def small_device(
    tokens,
    cotangent,
    expert_ids,
    attention_gain,
    query_gain,
    key_gain,
    query_weight,
    key_weight,
    value_weight,
    output_weight,
    expert_gain,
    router_weight,
    gate_weight,
    up_weight,
    down_weight,
):
    count, rows, width = tokens.shape
    hd = query_gain.shape[0]
    f = lax.axis_index("fsdp")
    n_fsdp = lax.axis_size("fsdp")
    seq = rows * n_fsdp
    experts = gate_weight.shape[0]
    expert_count = experts * n_fsdp
    piece = query_weight.shape[0]

    cosine, sine = signed_tables(seq, hd)
    inputs = tokens.astype(F32)
    input_hat, attention_factor = norm_parts(inputs)
    normed = (input_hat * attention_gain).astype(LOW)

    (normed_all, weights, output_pair, router_all, ids_all, grad_all, pre, qkv, prob, context, branch) = begin(
        normed,
        cotangent,
        query_weight,
        key_weight,
        value_weight,
        output_weight,
        router_weight.T,
        expert_ids.transpose(0, 2, 1),
        cosine,
        sine,
        query_gain,
        key_gain,
    )
    resid = inputs + branch.astype(F32)
    resid_hat, expert_factor = norm_parts(resid)
    expert_in = (resid_hat * expert_gain).astype(LOW)

    expert_all, act, dx_sum, out_sum, probs, dgp = run_experts(
        expert_in, grad_all, ids_all, router_all, gate_weight, up_weight, down_weight
    )
    layer_output = (resid + out_sum.astype(F32)).astype(LOW)
    dgp = dgp[:, :experts].reshape(expert_count, count * rows)
    d_logits = (probs * (dgp - jnp.sum(probs * dgp, axis=0, keepdims=True))).astype(LOW)
    d_expert_in = dx_sum.astype(F32) + lax.dot_general(
        d_logits, router_all, (((0,), (0,)), ((), ())), preferred_element_type=F32
    ).reshape(dx_sum.shape)
    router_part = jnp.dot(
        d_logits, expert_in.reshape(count * rows, width), preferred_element_type=F32
    )
    expert_gain_part = jnp.sum(d_expert_in * resid_hat, axis=(0, 1))
    out_grad = cotangent.astype(F32)
    d_resid = out_grad + norm_back(d_expert_in, expert_gain, resid_hat, expert_factor)
    d_branch = d_resid.astype(LOW)

    aux = jnp.concatenate(
        [
            router_part.reshape(expert_count, n_fsdp, piece).transpose(1, 0, 2),
            expert_gain_part.reshape(n_fsdp, 1, piece),
            jnp.zeros((n_fsdp, -(expert_count + 1) % 16, piece), F32),
        ],
        axis=1,
    ).astype(LOW)
    d_normed, d_query, d_key, d_value, d_output, aux_sum, line = end(
        d_branch,
        normed_all,
        weights,
        output_pair,
        pre,
        qkv,
        prob,
        context,
        aux,
        query_weight,
        key_weight,
        value_weight,
        cosine,
        sine,
        query_gain,
        key_gain,
    )
    input_grad = (
        d_resid + norm_back(d_normed.astype(F32), attention_gain, input_hat, attention_factor)
    ).astype(LOW)
    d_gate, d_up, d_down = expert_grads(act, expert_all, grad_all)
    own_gain = lax.dynamic_slice_in_dim(attention_gain, f * piece, piece, 0)
    head_piece = hd // n_fsdp
    head_gains = lax.dynamic_slice_in_dim(line[:2, piece:], f * head_piece, head_piece, 1)
    return (
        layer_output,
        input_grad,
        line[0, :piece] / own_gain,
        head_gains[0],
        head_gains[1],
        d_query,
        d_key,
        d_value,
        d_output,
        aux_sum[expert_count],
        aux_sum[:expert_count].T,
        d_gate.reshape(gate_weight.shape),
        d_up.reshape(up_weight.shape),
        d_down.reshape(down_weight.shape),
    )


def solution(mesh):
    body = small_device if (mesh.shape["fsdp"], mesh.shape["tp"]) == (8, 4) else general_device
    return jax.shard_map(
        body,
        mesh=mesh,
        in_specs=(
            P(None, "fsdp", None),
            P(None, "fsdp", None),
            P(None, "fsdp", None),
            P(),
            P(),
            P(),
            P("fsdp", "tp"),
            P("fsdp", "tp"),
            P("fsdp", "tp"),
            P("fsdp", "tp"),
            P(),
            P("fsdp", None),
            P("fsdp", "tp", None),
            P("fsdp", "tp", None),
            P("fsdp", "tp", None),
        ),
        out_specs=(
            P(None, "fsdp", None),
            P(None, "fsdp", None),
            P("fsdp"),
            P("fsdp"),
            P("fsdp"),
            P("fsdp", "tp"),
            P("fsdp", "tp"),
            P("fsdp", "tp"),
            P("fsdp", "tp"),
            P("fsdp"),
            P("fsdp", None),
            P("fsdp", "tp", None),
            P("fsdp", "tp", None),
            P("fsdp", "tp", None),
        ),
        check_vma=False,
    )
```

profile of v0, /device:TPU:16, one launch (start us, length us, event | category | flops | bytes accessed | tf_op | source)
XLA Modules:
  0.0 486.7 jit_solution(16573175848714595628)
XLA Ops:
  0.6 1.5 fusion.9
  2.2 2.5 fusion.3.normed
  4.7 138.9 %begin.1 = (bf16[1,1024,2048]{2,1,0:T(8,128)(2,1)}, bf16[2048,512]{1,0:T(8,128)(2,1)}, bf16[2048,256]{1,0:T(8,128)(2,1)}, bf16[32,2048]{1,0:T(8,128)(2,1)}, s32[...) custom-call(bf16[2,128,2048]{2,1,0:T(8,128)(2,1)} %fusion.3.normed, ...), custom_call_target="tpu_custom_call" | custom-call | tf_op jit(solution)/shard_map/begin/pallas_call | solution.py:617
  143.6 1.7 multiply_reduce_fusion.2
  145.4 1.5 multiply_convert_fusion.expert_in
  146.8 157.1 %experts.1 = (bf16[2,1024,2048]{2,1,0:T(8,128)(2,1)}, bf16[3,2,1024,768]{3,2,1,0:T(8,128)(2,1)}, bf16[2,128,2048]{2,1,0:T(8,128)(2,1)}, bf16[2,128,2048]{2,1,0:T...) custom-call(bf16[2,128,2048]{2,1,0:T(8,128)(2,1)} %multiply_convert_fusion.expert_in, ...), custom_call_target="tpu_custom_call" | custom-call | tf_op jit(solution)/shard_map/experts/pallas_call | solution.py:869
  303.9 0.8 slice.21
  304.8 0.9 multiply_reduce_fusion.3
  305.6 0.8 multiply_convert_fusion.1
  306.9 2.5 multiply_reduce_fusion
  309.4 2.1 fusion.13.d_branch
  311.5 2.4 copy.32
  313.9 1.6 fusion.11
  315.7 0.8 maximum_maximum_fusion.aux
  316.4 129.2 %end.1 = (bf16[2,128,2048]{2,1,0:T(8,128)(2,1)}, f32[256,1024]{1,0:T(8,128)}, f32[256,128]{1,0:T(8,128)}, f32[256,128]{1,0:T(8,128)}, f32[256,1024]{1,0:T(8,128)}, /*index=5*/f32[48,256]{1,0:T(8,128)}, f32[8,384]{1,0:T(8,128)}) custom-call(bf16[2,128,2048]{2,1,0:T(8,128)(2,1)} %fusion.13.d_branch, bf16[1,1024,2048]{2,1,0:T(8,128)(2,1)} %get-tuple-element.49.xn_in, ...), custom_call_target="tpu_custom_call" | custom-call | tf_op jit(solution)/shard_map/end/pallas_call | solution.py:1138
  445.6 1.9 fusion.4
  447.6 5.0 %fusion.8 = (bf16[2,128,2048]{2,1,0:T(8,128)(2,1)}, bf16[2,128,2048]{2,1,0:T(8,128)(2,1)}) fusion(bf16[2,128,2048]{2,1,0:T(8,128)(2,1)S(1)} %copy-done, bf16[2,128,2048]{2,1,0:T(8,128)(2,1)} %get-tuple-element.56, f32[2,128]{1,0:T(2,128)S(1)} %broadcast_multiply_fusion, f32[2048]{0:T(1024)S(1)} %copy-done.13, f32[2,128]{1,0:T(2,128)S(1)} %add_rsqrt_fusion.1, ...), kind=kLoop, calls=%fused_computation.11 | loop fusion | flops 12058624 | bytes 10506240 | tf_op jit(solution)/shard_map/convert_element_type | solution.py:1746
  452.6 0.7 slice.22
  453.9 0.7 slice.23
  456.4 26.5 %expert_grads.1 = (f32[768,2048]{1,0:T(8,128)}, f32[768,2048]{1,0:T(8,128)}, f32[768,2048]{1,0:T(8,128)}) custom-call(bf16[3,2,1024,768]{3,2,1,0:T(8,128)(2,1)} %get-tuple-element.63.act, bf16[2,1024,2048]{2,1,0:T(8,128)(2,1)} %get-tuple-element.64.x, bf16[2,1024,2048]{2,1,0:T(8,128)(2,1)} %get-tuple-element.42.og_in.og), custom_call_target="tpu_custom_call" | custom-call | tf_op jit(solution)/shard_map/expert_grads/pallas_call | solution.py:932
  483.0 1.0 copy.38
  483.9 0.7 copy.39
  484.6 0.7 copy.40
  485.3 1.0 copy.41
  (44 shorter events, 3.1 us)
Async XLA Ops:
  4.7 138.9 %copy-start = (bf16[2,128,2048]{2,1,0:T(8,128)(2,1)S(1)}, bf16[2,128,2048]{2,1,0:T(8,128)(2,1)}, u32[]{:S(2)}) copy-start(bf16[2,128,2048]{2,1,0:T(8,128)(2,1)} %param.17) | copy-start | bytes 3145732
  143.6 1.8 copy-start.1
  143.6 1.8 copy-start.10
  146.8 159.6 %copy-start.9 = (bf16[32,2048]{1,0:T(8,128)(2,1)S(1)}, bf16[32,2048]{1,0:T(8,128)(2,1)}, u32[]{:S(2)}) copy-start(bf16[32,2048]{1,0:T(8,128)(2,1)} %get-tuple-element.44.router) | copy-start | bytes 393220
  304.8 2.1 copy-start.6
  306.9 2.5 copy-start.2
  306.9 2.5 copy-start.4
  316.4 129.2 %copy-start.13 = (f32[2048]{0:T(1024)S(1)}, f32[2048]{0:T(1024)}, u32[]{:S(2)}) copy-start(f32[2048]{0:T(1024)} %param.20) | copy-start | bytes 24580
  445.6 2.0 copy-start.3
  445.6 2.0 copy-start.5
  447.6 7.7 %copy-start.14 = (f32[48,256]{1,0:T(8,128)S(1)}, f32[48,256]{1,0:T(8,128)}, u32[]{:S(2)}) copy-start(f32[48,256]{1,0:T(8,128)} %get-tuple-element.62) | copy-start | bytes 147460
  456.4 26.6 %copy-start.8 = (f32[256,1024]{1,0:T(8,128)S(1)}, f32[256,1024]{1,0:T(8,128)}, u32[]{:S(2)}) copy-start(f32[256,1024]{1,0:T(8,128)} %get-tuple-element.93) | copy-start | bytes 3145732
  482.9 1.0 copy-start.12
  482.9 1.7 copy-start.11
  482.9 2.3 copy-start.7
where the time goes:
time: 494 us; the launch traced here: 487 us
  Pallas kernels  452 us (91%)
  other arithmetic  21.8 us (4%)
  local copies, waits for them, and re-layouts  9.89 us (2%)
    pallas_call x1, Pallas kernels, run_experts(): pl.pallas_call(functools.partial(experts_kernel, experts), out_shape=(sha...  157 us
    pallas_call x1, Pallas kernels, begin(): pl.pallas_call(functools.partial(begin_kernel, heads), out_shape=(shape(*...  139 us
    pallas_call x1, Pallas kernels, end(): pl.pallas_call(functools.partial(end_kernel, heads), out_shape=(shape((co...  129 us
    pallas_call x1, Pallas kernels, expert_grads(): pl.pallas_call(expert_grads_kernel, grid=(width // block,), in_specs=[pl....  26.5 us

commit v1 on v0

--- a/solution.py
+++ b/solution.py
@@ -15,7 +15,7 @@
 MESH = pl.DeviceIdType.MESH
 LOW = jnp.bfloat16
 F32 = jnp.float32
-VMEM_LIMIT = 60 * 2**20
+VMEM_LIMIT = 62 * 2**20
 
 
 def coords():
@@ -235,14 +235,15 @@
 def add_into(target, *others):
     count, rows, _ = target.shape
     step = 32
+    wide = target.dtype if len(others) == 1 else F32
 
     @pl.loop(0, count * rows // step)
     def _(i):
         n = i // (rows // step)
         r = pl.ds(pl.multiple_of((i % (rows // step)) * step, step), step)
-        total = target[n, r, :].astype(F32)
+        total = target[n, r, :].astype(wide)
         for other in others:
-            total = total + other[n, r, :].astype(F32)
+            total = total + other[n, r, :].astype(wide)
         target[n, r, :] = total.astype(target.dtype)
 
 
@@ -376,6 +377,8 @@
         self.landed(self.full.at[2 * h.y + 1 - h.c], self.rg.at[1])
         self.landed(self.full.at[2 * (1 - h.y) + 1 - h.c], self.rg.at[2])
         self.keeps[0].wait()
+        if out is None:
+            return
         outs = [keep(self.full.at[q], out.at[:, :, pl.ds(q * self.cols, self.cols)], self.osem.at[q]) for q in range(4)]
         for copy in outs:
             copy.wait()
@@ -491,10 +494,27 @@
             copy.wait_send()
 
 
-def begin_kernel(heads, normed, cot, query, key, value, output, router, ids, cos_ref, sin_ref, qg_ref, kg_ref,
-                 xn_out, w_out, wo_out, router_out, ids_out, cot_out, pre_out, qkv_out, prob_out, ctx_out, branch_out,
-                 xn, w, wo, pre, qkv, prob, ctx, part, own, osem, *sems):
+def unit(values):
+    factor = lax.rsqrt(jnp.mean(values * values, axis=-1, keepdims=True) + norm_eps)
+    return values * factor, factor
+
+
+def begin_kernel(heads, cot, query, key, value, output, router, ids, tokens, ag_ref, eg_ref,
+                 cos_ref, sin_ref, qg_ref, kg_ref, xn_out, w_out, wo_out, router_out, ids_out, cot_out, pre_out, qkv_out, prob_out, ctx_out, resid_out, expert_out,
+                 normed, resid, xn, w, wo, pre, qkv, prob, ctx, part, own, osem, *sems):
     here = Here()
+    count, rows, _ = tokens.shape
+    step = 32
+    steps = rows // step
+
+    def chunk_of(i):
+        return i // steps, pl.ds(pl.multiple_of(i % steps * step, step), step)
+
+    @pl.loop(0, count * steps)
+    def _(i):
+        n, r = chunk_of(i)
+        normed[n, r, :] = (unit(tokens[n, r, :].astype(F32))[0] * ag_ref[...]).astype(LOW)
+
     here.greet()
     at = 0
     x_rows = Gather(here, False, normed, xn, sems[at : at + Gather.slots], BY_X)
@@ -558,7 +578,6 @@
     outs += [keep(prob, prob_out, osem.at[4]), keep(ctx, ctx_out, osem.at[5])]
     moved.wait_pairs(1)
     outs.append(keep(wo, wo_out, osem.at[6]))
-    rows = total.rows
     for e in (1, 0):
         for d in FAR_FIRST:
             at_f = span(here.number(d, e) * rows, rows)
@@ -585,18 +604,30 @@
     c_rows.close(2)
     total.share_cross()
     c_rows.close(3)
-    total.share_end(branch_out)
+    total.share_end(None)
+    x_rows.finish()
+
+    @pl.loop(0, count * steps)
+    def _(i):
+        n, r = chunk_of(i)
+        branch = jnp.concatenate([total.full[q, n, r, :] for q in range(4)], axis=1).astype(F32)
+        summed = tokens[n, r, :].astype(F32) + branch
+        resid[n, r, :] = summed
+        normed[n, r, :] = (unit(summed)[0] * eg_ref[...]).astype(LOW)
+
+    outs += [keep(resid, resid_out, osem.at[7]), keep(normed, expert_out, osem.at[8])]
     for d in (0,) + ORDER:
         c_rows.arrived(d, 0)
         c_rows.arrived(d, 1)
-    for each in (x_rows, c_rows, moved, total):
+    for each in (c_rows, moved, total):
         each.finish()
     for copy in outs:
         copy.wait()
 
 
-def begin(normed, cot, query, key, value, output, router, ids, cosine, sine, query_gain, key_gain):
-    count, rows, width = normed.shape
+def begin(cot, query, key, value, output, router, ids, tokens, attention_gain, expert_gain,
+          cosine, sine, query_gain, key_gain):
+    count, rows, width = tokens.shape
     seq = rows * 8
     hd = query_gain.shape[0]
     part = query.shape[1] // 4
@@ -627,18 +658,21 @@
             shape(*local[4]),
             shape(*local[5]),
             shape(*local[6]),
+            shape((count, rows, width), F32),
             shape((count, rows, width), LOW),
         ),
-        in_specs=[hbm] * 8 + [near] * 4,
-        out_specs=[hbm] * 11,
-        scratch_shapes=[vm(*entry) for entry in local]
-        + [vm((1, seq, width), LOW), vm((count, rows, width), LOW), pltpu.SemaphoreType.DMA((7,))]
+        in_specs=[hbm] * 7 + [near] * 7,
+        out_specs=[hbm] * 12,
+        scratch_shapes=[vm((count, rows, width), LOW), vm((count, rows, width), F32)]
+        + [vm(*entry) for entry in local]
+        + [vm((1, seq, width), LOW), vm((count, rows, width), LOW), pltpu.SemaphoreType.DMA((9,))]
         + Gather.scratch() + Gather.scratch() + Weights.scratch() + Sum.scratch(1, rows, width, LOW, BY_X),
         compiler_params=pltpu.CompilerParams(
             collective_id=4, has_side_effects=True, vmem_limit_bytes=VMEM_LIMIT
         ),
         name="begin",
-    )(normed, cot, query, key, value, output, router, ids, cosine, sine, query_gain[None], key_gain[None])
+    )(cot, query, key, value, output, router, ids, tokens, attention_gain[None], expert_gain[None],
+      cosine, sine, query_gain[None], key_gain[None])
 
 
 def experts_kernel(experts, expert_in, og_in, ids, router, g_in, u_in, d_in,
@@ -648,7 +682,7 @@
     here = Here()
     here.greet()
     by_x = expert_in.shape[1] // 2
-    rows_x = Gather(here, True, expert_in, x_out, rest[: Gather.slots], by_x, x_t)
+    rows_x = Gather(here, True, expert_in, x_out, rest[: Gather.slots], by_x, x_t.at[0])
     sums = (
         Sum(here, True, dx, rest[Gather.slots : Gather.slots + Sum.slots], by_x),
         Sum(here, True, out, rest[Gather.slots + Sum.slots :], by_x),
@@ -664,45 +698,50 @@
     rows_x.start()
     loads = [keep(src, dst, wsem.at[n]) for n, (src, dst) in enumerate(((d_in, dn), (g_in, g), (u_in, u)))]
 
+    def plane(i):
+        k = i // 2
+        return k + (k + 2) // 3 - 3 * (k // 3)
+
     def tile(i):
-        return span(number(i // 2, i % 2) * rows, rows)
+        return span(number(plane(i), i % 2) * rows, rows)
 
     def og_load(i):
         return pltpu.make_async_copy(og_in.at[:, tile(i), :], og_t.at[i % 2], ogsem.at[i % 2])
 
     def x_load(i):
-        return pltpu.make_async_copy(x_out.at[:, tile(i), :], x_t, xsem.at[0])
+        return pltpu.make_async_copy(x_out.at[:, tile(i), :], x_t.at[i % 2], xsem.at[i % 2])
 
     def act_store(i):
         return pltpu.make_async_copy(act_t.at[i % 2], act_out.at[:, :, tile(i), :], actsem.at[i % 2])
 
     def dgp_send(i):
-        to = place(here.zd(i // 2), (here.x + i % 2) % 2, here.y, here.c)
+        to = place(here.zd(plane(i)), (here.x + i % 2) % 2, here.y, here.c)
         return remote(dgp_t.at[i], dgp_got.at[here.f], psem.at[i], rsem.at[here.f], to)
 
     def both(step, j):
         for each in sums:
             getattr(each, step)(j)
 
+    first = {2: lambda: (rows_x.relay(1), rows_x.spread(1))}
     early = {
-        2: lambda: (rows_x.relay(1), rows_x.spread(1)),
-        4: lambda: (rows_x.cross(0),),
-        6: lambda: (rows_x.relay(2), rows_x.spread(2)),
+        3: lambda: (rows_x.cross(0),),
+        5: lambda: (rows_x.relay(2), rows_x.spread(2)),
         7: lambda: (rows_x.cross(1), rows_x.close(0)),
     }
     before = {
         1: lambda: (rows_x.relay(3), rows_x.spread(3), rows_x.arrived(0, 1)),
-        2: lambda: (rows_x.arrived(1, 0), rows_x.arrived(1, 1)),
+        2: lambda: (rows_x.close(2), rows_x.arrived(2, 0), rows_x.arrived(2, 1)),
         3: lambda: (both("corner", 0),),
-        4: lambda: (rows_x.arrived(2, 0), rows_x.arrived(2, 1)),
-        5: lambda: (both("sides", 0), both("corner", 1)),
-        6: lambda: (rows_x.arrived(3, 0), rows_x.arrived(3, 1)),
-        7: lambda: (both("sides", 1), both("corner", 2), both("centre", 0)),
+        5: lambda: (both("corner", 2),),
+        7: lambda: (both("corner", 3),),
     }
     middle = {
         1: lambda: (rows_x.cross(2), rows_x.close(1)),
-        2: lambda: (rows_x.cross(3), rows_x.close(2)),
-        3: lambda: (rows_x.close(3),),
+        2: lambda: (rows_x.cross(3),),
+        3: lambda: (rows_x.close(3), rows_x.arrived(3, 0), rows_x.arrived(3, 1)),
+        4: lambda: (both("sides", 0),),
+        5: lambda: (rows_x.arrived(1, 0), rows_x.arrived(1, 1)),
+        6: lambda: (both("sides", 2), both("centre", 0)),
     }
 
     def hooks(table, i):
@@ -719,7 +758,7 @@
     gather8 = jnp.where(row8 == col8 // per, 1.0, 0.0).astype(LOW)
 
     def first_half(i):
-        x_tile = x_t[...].reshape(tokens, width)
+        x_tile = x_t[i % 2].reshape(tokens, width)
         for n, right in enumerate((g, u)):
             for k in range(hidden // part):
                 stage[n, pl.ds(k * tokens, tokens), :] = dot_nt(x_tile, right[pl.ds(k * part, part), :])
@@ -732,9 +771,7 @@
         masked = jnp.where(named, logits, masked_score)
         terms = jnp.where(named, jnp.exp(masked - jnp.max(masked, axis=0, keepdims=True)), 0.0)
         probs = terms / jnp.sum(terms, axis=0, keepdims=True)
-        high = probs.astype(LOW)
-        low = (probs - high.astype(F32)).astype(LOW)
-        share_s[...] = dot_tn(high, spread) + dot_tn(low, spread)
+        share_s[...] = dot_tn(probs.astype(LOW), spread)
         return probs
 
     def between(i, m):
@@ -748,10 +785,7 @@
         sig = 1.0 / (1.0 + jnp.exp(-gate))
         silu = gate * sig
         inner = silu * up
-        product = inner * raw
-        product_high = product.astype(LOW)
-        product_low = (product - product_high.astype(F32)).astype(LOW)
-        dgp_t[i, :, r] = dot_nt(gather8, product_high) + dot_nt(gather8, product_low)
+        dgp_t[i, :, r] = dot_nt(gather8, (inner * raw).astype(LOW))
         d_inner = raw * share
         act_t[i % 2, 0, m] = (d_inner * up * (sig + silu * (1.0 - sig))).astype(LOW)
         act_t[i % 2, 1, m] = (d_inner * silu).astype(LOW)
@@ -766,7 +800,7 @@
 
     def sent(i):
         for each in sums:
-            each.give(i // 2, i % 2)
+            each.give(plane(i), i % 2)
 
         @pl.when(i > 0)
         def _():
@@ -775,16 +809,16 @@
     og_load(0).start()
     loads[0].wait()
 
-    @pl.loop(0, 8)
-    def _(i):
+    def raw_step(table, i):
         @pl.when(i + 1 < 8)
         def _():
             og_load(i + 1).start()
 
-        hooks(early, i)
+        hooks(table, i)
         og_load(i).wait()
         raw_s[i] = dot_nt(og_t[i % 2].reshape(tokens, width), dn[...]).astype(LOW)
 
+    pl.loop(0, 3)(functools.partial(raw_step, first))
     loads[1].wait()
     loads[2].wait()
     rows_x.arrived(0, 0)
@@ -792,11 +826,15 @@
     for m in range(count):
         between(0, m)
     act_store(0).start()
+    pl.loop(3, 8)(functools.partial(raw_step, early))
 
     @pl.loop(1, 8)
     def _(i):
         hooks(before, i)
-        x_load(i).start()
+
+        @pl.when(i < 3)
+        def _():
+            x_load(i).start()
 
         @pl.when(i >= 2)
         def _():
@@ -805,6 +843,11 @@
         x_load(i).wait()
         first_half(i)
         hooks(middle, i)
+
+        @pl.when((i >= 2) & (i < 7))
+        def _():
+            x_load(i + 1).start()
+
         for m in range(count):
             second_half(i - 1, 2 * m)
             between(i, m)
@@ -815,12 +858,18 @@
     for q in range(4):
         second_half(7, q)
     sent(7)
-    both("corner", 3)
-    both("sides", 2)
-    both("centre", 1)
-    both("sides", 3)
-    both("centre", 2)
-    both("centre", 3)
+    ahead, behind = sums
+    ahead.corner(1)
+    ahead.sides(3)
+    ahead.centre(2)
+    behind.corner(1)
+    behind.sides(3)
+    ahead.sides(1)
+    ahead.centre(3)
+    behind.centre(2)
+    behind.sides(1)
+    ahead.centre(1)
+    behind.centre(3)
     for d in range(4):
         for e in range(2):
             if d or e:
@@ -828,19 +877,20 @@
                 wait_for(dgp_got.at[n], rsem.at[n], here.xn)
                 dgp_all[n] = dgp_got[n]
     dgp_all[here.f] = dgp_t[0]
-    first = push(dgp_all, dgp_c, tsem.at[0], usem.at[0], here.cn)
-    sums[0].total()
+    across = push(dgp_all, dgp_c, tsem.at[0], usem.at[0], here.cn)
+    ahead.total()
+    ahead.share_start()
+    behind.centre(1)
     wait_for(dgp_c, usem.at[0], here.cn)
-    first.wait_send()
+    across.wait_send()
     dgp_all[...] = dgp_all[...] + dgp_c[...]
     second = push(dgp_all, dgp_y, tsem.at[1], usem.at[1], here.yn)
-    sums[0].share_start()
-    sums[1].total()
-    sums[1].share_start()
-    sums[0].share_cross()
-    sums[1].share_cross()
-    sums[0].share_end(dx_sum)
-    sums[1].share_end(out_sum)
+    ahead.share_cross()
+    behind.total()
+    behind.share_start()
+    ahead.share_end(dx_sum)
+    behind.share_cross()
+    behind.share_end(out_sum)
     wait_for(dgp_y, usem.at[1], here.yn)
     dgp_out[...] = dgp_all[...] + dgp_y[...]
     second.wait_send()
@@ -879,7 +929,7 @@
         in_specs=[hbm, hbm, near, near, hbm, hbm, hbm],
         out_specs=[hbm, hbm, hbm, hbm, near, near],
         scratch_shapes=[
-            vm((count, rows, width), LOW),
+            vm((2, count, rows, width), LOW),
             vm((hidden, width), LOW),
             vm((hidden, width), LOW),
             vm((hidden, width), LOW),
@@ -897,7 +947,7 @@
             vm((8, 8, tokens), F32),
             dma((3,)),
             dma((2,)),
-            dma((1,)),
+            dma((2,)),
             dma((2,)),
             dma((8,)),
             dma((8,)),
@@ -914,49 +964,62 @@
     )(expert_in, og, ids, router, gate.reshape(hidden, width), up.reshape(hidden, width), down.reshape(hidden, width))
 
 
-def expert_grads_kernel(act, x, og, dg, du, dd):
+def expert_grads_kernel(act, x, og, *refs):
+    kept = (len(refs) - 3) // 2
     tokens = act.shape[1] * act.shape[2]
     x_cols = x[...].reshape(tokens, x.shape[2])
     og_cols = og[...].reshape(tokens, og.shape[2])
-    for n, (right, out) in enumerate(((x_cols, dg), (x_cols, du), (og_cols, dd))):
-        out[...] = dot_tn(act[n].reshape(tokens, act.shape[3]), right)
-
-
-def expert_grads(act, x, og):
+    for n, right in enumerate((x_cols, x_cols, og_cols)):
+        refs[kept + n][...] = dot_tn(act[n].reshape(tokens, act.shape[3]), right)
+    for src, dst in zip(refs[:kept], refs[kept + 3 :]):
+        dst[...] = src[...]
+
+
+def expert_grads(act, x, og, *others):
     _, count, seq, hidden = act.shape
     width = x.shape[2]
     block = min(512, width)
+    steps = width // block
     cols = pl.BlockSpec((count, seq, block), lambda i: (0, 0, i))
     out = pl.BlockSpec((hidden, block), lambda i: (0, i))
+
+    def pieces(value):
+        shape = value.shape[:-2] + (value.shape[-2] // steps, value.shape[-1])
+        zeros = (0,) * (len(shape) - 2)
+        return pl.BlockSpec(shape, lambda i: zeros + (i, 0))
+
     grads = jax.ShapeDtypeStruct((hidden, width), F32)
+    kept = [pieces(value) for value in others]
     return pl.pallas_call(
         expert_grads_kernel,
-        grid=(width // block,),
+        grid=(steps,),
         in_specs=[
             pl.BlockSpec(act.shape, lambda i: (0, 0, 0, 0), pipeline_mode=pl.Buffered(1)),
             cols,
             cols,
-        ],
-        out_specs=[out, out, out],
-        out_shape=(grads, grads, grads),
+        ]
+        + kept,
+        out_specs=[out, out, out] + kept,
+        out_shape=[grads] * 3 + [jax.ShapeDtypeStruct(value.shape, value.dtype) for value in others],
         compiler_params=pltpu.CompilerParams(vmem_limit_bytes=VMEM_LIMIT),
         name="expert_grads",
-    )(act, x, og)
+    )(act, x, og, *others)
 
 
 PEERS = tuple((d, e) for d in (2, 1, 3, 0) for e in (1, 0) if d or e)
 
 
-def end_kernel(heads, d_branch, xn_in, w_in, wo_in, pre_in, qkv_in, prob_in, ctx_in, aux, query, key, value,
+def end_kernel(heads, xn_in, w_in, wo_in, pre_in, qkv_in, prob_in, ctx_in, tokens_in, out_in,
+               resid, cot, dx_sum, expert_in, probs, dgp, router, eg_ref, ag_ref, query, key, value,
                cos_ref, sin_ref, qg_ref, kg_ref,
-               dn_sum, dq_out, dk_out, dv_out, do_out, aux_out, gains_out,
-               db, xn, w, wo, pre, qkv, prob, ctx, dctx, dq_s, dk_s, dv_s, dqkv, dwo, dw, dwo_got, dwq_got, kv_x, kv_z,
+               layer_out, input_out, dq_out, dk_out, dv_out, do_out, aux_out, gains_out,
+               tokens, out_sum, d_res, low_rows, layer, aux, db, xn, w, wo, pre, qkv, prob, ctx, dctx, dq_s, dk_s, dv_s, dqkv, dwo, dw, dwo_got, dwq_got, kv_x, kv_z,
                aux_got, head_part, head_got, line, line_c, line_y, wide_q, wide_o, wide_kv,
                lsem, psem, rsem, kxs, kxr, kzs, kzr, tsem, usem, osem, *rest):
     here = Here()
     here.greet()
     sends, outs = [], []
-    rows_db = Gather(here, False, d_branch, db, rest[: Gather.slots], BY_X)
+    rows_db = Gather(here, False, low_rows, db, rest[: Gather.slots], BY_X)
     at = Gather.slots
     dn = Sum(here, False, db, rest[at:], BY_X)
     rows = dn.rows
@@ -976,11 +1039,45 @@
         wait_for(got.at[d, e], rsem.at[n, d, e], here.xn)
         return got[d, e]
 
-    rows_db.start()
     loads = {}
     for n, (src, dst) in enumerate(((wo_in, wo), (ctx_in, ctx), (qkv_in, qkv), (prob_in, prob), (pre_in, pre),
-                                    (xn_in, xn), (w_in, w))):
+                                    (xn_in, xn), (w_in, w), (tokens_in, tokens), (out_in, out_sum))):
         loads[n] = keep(src, dst, lsem.at[n])
+    count, lanes, width = resid.shape[0], probs.shape[0], resid.shape[2]
+    experts = lanes // 8
+    step = 32
+    steps = rows // step
+
+    def chunk_of(i):
+        return i // steps, pl.ds(pl.multiple_of(i % steps * step, step), step)
+
+    def unit_back(up, gain, hat, factor):
+        gained = up * gain
+        return factor * (gained - hat * jnp.mean(gained * hat, axis=-1, keepdims=True))
+
+    d_probs = jnp.concatenate([dgp[k, :experts, :] for k in range(8)], axis=0)
+    mixed = probs[...] * d_probs
+    d_logits = (mixed - probs[...] * jnp.sum(mixed, axis=0, keepdims=True)).astype(LOW)
+    for n in range(count):
+        d_res[n] = dot_tn(d_logits[:, n * rows : (n + 1) * rows], router[...])
+
+    def back(i, gain_part):
+        n, r = chunk_of(i)
+        hat, factor = unit(resid[n, r, :])
+        d_in = d_res[n, r, :] + dx_sum[n, r, :].astype(F32)
+        total = cot[n, r, :].astype(F32) + unit_back(d_in, eg_ref[...], hat, factor)
+        d_res[n, r, :] = total
+        low_rows[n, r, :] = total.astype(LOW)
+        return gain_part + jnp.sum(d_in * hat, axis=0, keepdims=True)
+
+    gain_part = lax.fori_loop(0, count * steps, back, jnp.zeros((1, width), F32))
+    rows_db.start()
+    router_part = dot_nn(d_logits, expert_in[...].reshape(count * rows, width)).astype(LOW)
+    first_row = lax.broadcasted_iota(jnp.int32, (16, piece), 0) == 0
+    for k in range(8):
+        cols = slice(k * piece, (k + 1) * piece)
+        aux[k, pl.ds(0, lanes), :] = router_part[:, cols]
+        aux[k, pl.ds(lanes, 16), :] = jnp.where(first_row, gain_part[:, cols], 0.0).astype(LOW)
     for d, e in PEERS:
         send(0, d, e, aux.at[number(d, e)], aux_got)
     rows_db.first_steps()
@@ -988,7 +1085,7 @@
     for d in (0,) + ORDER:
         rows_db.arrived(d, 0)
         rows_db.arrived(d, 1)
-    for n in range(7):
+    for n in range(9):
         loads[n].wait()
 
     for i in range(seq // tile):
@@ -999,6 +1096,12 @@
         dwo[r, :] = dot_tn(db[0, :, r], ctx[...]).astype(LOW)
         if d or e:
             send(1, d, e, dwo.at[r, :], dwo_got)
+    @pl.loop(0, count * steps)
+    def _(i):
+        n, r = chunk_of(i)
+        layer[n, r, :] = (resid[n, r, :] + out_sum[n, r, :].astype(F32)).astype(LOW)
+
+    outs.append(keep(layer, layer_out, osem.at[4]))
     dk_s[...] = jnp.zeros_like(dk_s)
     dv_s[...] = jnp.zeros_like(dv_s)
     for a in range(heads):
@@ -1086,7 +1189,18 @@
         head_total = head_total + got_from(3, d, e, head_got)
     line[:, pl.ds(piece, hd)] = head_total
     dn.total()
-    dn.share(dn_sum)
+    dn.share_start()
+    dn.share_cross()
+    dn.share_end(None)
+
+    @pl.loop(0, count * steps)
+    def _(i):
+        n, r = chunk_of(i)
+        hat, factor = unit(tokens[n, r, :].astype(F32))
+        up = jnp.concatenate([dn.full[q, n, r, :] for q in range(4)], axis=1).astype(F32)
+        low_rows[n, r, :] = (d_res[n, r, :] + unit_back(up, ag_ref[...], hat, factor)).astype(LOW)
+
+    outs.append(keep(low_rows, input_out, osem.at[5]))
     merged(2, wide_q, dwq_got, dw[own, pl.ds(0, part)])
     outs.append(keep(wide_q, dq_out, osem.at[1]))
     kv = dw[own, pl.ds(part, 2 * hd)].astype(F32)
@@ -1123,9 +1237,11 @@
         copy.wait()
 
 
-def end(d_branch, xn, w, wo, pre, qkv, prob, ctx, aux, query, key, value, cosine, sine, query_gain, key_gain):
-    count, rows, width = d_branch.shape
+def end(xn, w, wo, pre, qkv, prob, ctx, tokens, out_sum, resid, cot, dx_sum, expert_in, probs, dgp, router,
+        expert_gain, attention_gain, query, key, value, cosine, sine, query_gain, key_gain):
+    count, rows, width = tokens.shape
     seq = rows * 8
+    lanes = probs.shape[0]
     hd = query_gain.shape[0]
     piece, local = query.shape
     part = local // 4
@@ -1139,16 +1255,23 @@
         functools.partial(end_kernel, heads),
         out_shape=(
             shape((count, rows, width), LOW),
+            shape((count, rows, width), LOW),
             shape((piece, local), F32),
             shape((piece, hd), F32),
             shape((piece, hd), F32),
             shape((piece, local), F32),
-            shape(aux.shape[1:], F32),
+            shape((lanes + 16, piece), F32),
             shape((8, piece + hd), F32),
         ),
-        in_specs=[hbm] * 8 + [near] * 8,
-        out_specs=[hbm] * 5 + [near] * 2,
+        in_specs=[hbm] * 9 + [near] * 16,
+        out_specs=[hbm] * 6 + [near] * 2,
         scratch_shapes=[
+            vm((count, rows, width), LOW),
+            vm((count, rows, width), LOW),
+            vm((count, rows, width), F32),
+            vm((count, rows, width), LOW),
+            vm((count, rows, width), LOW),
+            vm((8, lanes + 16, piece), LOW),
             vm((1, seq, width), LOW),
             vm((1, seq, width), LOW),
             vm(w.shape, LOW),
@@ -1168,7 +1291,7 @@
             vm((4, 2, piece, part), LOW),
             vm((4, piece, 2 * hd), LOW),
             vm((4, piece, 2 * hd), LOW),
-            vm((4, 2) + aux.shape[1:], LOW),
+            vm((4, 2, lanes + 16, piece), LOW),
             vm((8, hd), F32),
             vm((4, 2, 8, hd), F32),
             vm((8, piece + hd), F32),
@@ -1177,7 +1300,7 @@
             vm((piece, local), F32),
             vm((piece, local), F32),
             vm((piece, 2 * hd), F32),
-            dma((7,)),
+            dma((9,)),
             dma((4, 4, 2)),
             dma((4, 4, 2)),
             dma((4,)),
@@ -1186,7 +1309,7 @@
             dma((4,)),
             dma((2,)),
             dma((2,)),
-            dma((4,)),
+            dma((6,)),
         ]
         + Gather.scratch()
         + Sum.scratch(1, rows, width, LOW, BY_X),
@@ -1194,8 +1317,8 @@
             collective_id=5, has_side_effects=True, vmem_limit_bytes=VMEM_LIMIT
         ),
         name="end",
-    )(d_branch, xn, w, wo, pre, qkv, prob, ctx, aux, query, key, value, cosine, sine,
-      query_gain[None], key_gain[None])
+    )(xn, w, wo, pre, qkv, prob, ctx, tokens, out_sum, resid, cot, dx_sum, expert_in, probs, dgp, router,
+      expert_gain[None], attention_gain[None], query, key, value, cosine, sine, query_gain[None], key_gain[None])
 
 
 def rotate_half(values):
@@ -1676,12 +1799,7 @@
     piece = query_weight.shape[0]
 
     cosine, sine = signed_tables(seq, hd)
-    inputs = tokens.astype(F32)
-    input_hat, attention_factor = norm_parts(inputs)
-    normed = (input_hat * attention_gain).astype(LOW)
-
-    (normed_all, weights, output_pair, router_all, ids_all, grad_all, pre, qkv, prob, context, branch) = begin(
-        normed,
+    (normed_all, weights, output_pair, router_all, ids_all, grad_all, pre, qkv, prob, context, resid, expert_in) = begin(
         cotangent,
         query_weight,
         key_weight,
@@ -1689,42 +1807,18 @@
         output_weight,
         router_weight.T,
         expert_ids.transpose(0, 2, 1),
+        tokens,
+        attention_gain,
+        expert_gain,
         cosine,
         sine,
         query_gain,
         key_gain,
     )
-    resid = inputs + branch.astype(F32)
-    resid_hat, expert_factor = norm_parts(resid)
-    expert_in = (resid_hat * expert_gain).astype(LOW)
-
     expert_all, act, dx_sum, out_sum, probs, dgp = run_experts(
         expert_in, grad_all, ids_all, router_all, gate_weight, up_weight, down_weight
     )
-    layer_output = (resid + out_sum.astype(F32)).astype(LOW)
-    dgp = dgp[:, :experts].reshape(expert_count, count * rows)
-    d_logits = (probs * (dgp - jnp.sum(probs * dgp, axis=0, keepdims=True))).astype(LOW)
-    d_expert_in = dx_sum.astype(F32) + lax.dot_general(
-        d_logits, router_all, (((0,), (0,)), ((), ())), preferred_element_type=F32
-    ).reshape(dx_sum.shape)
-    router_part = jnp.dot(
-        d_logits, expert_in.reshape(count * rows, width), preferred_element_type=F32
-    )
-    expert_gain_part = jnp.sum(d_expert_in * resid_hat, axis=(0, 1))
-    out_grad = cotangent.astype(F32)
-    d_resid = out_grad + norm_back(d_expert_in, expert_gain, resid_hat, expert_factor)
-    d_branch = d_resid.astype(LOW)
-
-    aux = jnp.concatenate(
-        [
-            router_part.reshape(expert_count, n_fsdp, piece).transpose(1, 0, 2),
-            expert_gain_part.reshape(n_fsdp, 1, piece),
-            jnp.zeros((n_fsdp, -(expert_count + 1) % 16, piece), F32),
-        ],
-        axis=1,
-    ).astype(LOW)
-    d_normed, d_query, d_key, d_value, d_output, aux_sum, line = end(
-        d_branch,
+    layer_output, input_grad, d_query, d_key, d_value, d_output, aux_sum, line = end(
         normed_all,
         weights,
         output_pair,
@@ -1732,7 +1826,17 @@
         qkv,
         prob,
         context,
-        aux,
+        tokens,
+        out_sum,
+        resid,
+        cotangent,
+        dx_sum,
+        expert_in,
+        probs,
+        dgp,
+        router_all,
+        expert_gain,
+        attention_gain,
         query_weight,
         key_weight,
         value_weight,
@@ -1741,10 +1845,9 @@
         query_gain,
         key_gain,
     )
-    input_grad = (
-        d_resid + norm_back(d_normed.astype(F32), attention_gain, input_hat, attention_factor)
-    ).astype(LOW)
-    d_gate, d_up, d_down = expert_grads(act, expert_all, grad_all)
+    d_gate, d_up, d_down, layer_output, input_grad, d_query, d_output = expert_grads(
+        act, expert_all, grad_all, layer_output, input_grad, d_query, d_output
+    )
     own_gain = lax.dynamic_slice_in_dim(attention_gain, f * piece, piece, 0)
     head_piece = hd // n_fsdp
     head_gains = lax.dynamic_slice_in_dim(line[:2, piece:], f * head_piece, head_piece, 1)

time: 494 us -> 470 us (0.951)
  other arithmetic: 21.8 us -> 1.33 us
  local copies, waits for them, and re-layouts: 9.89 us -> 4.47 us
    convert_element_type x5 -> x0, other arithmetic: 11.8 us -> none  [the longest x1 5.02 us: small_device(): input_grad = (d_resid + norm_back(d_normed.astype(F32), attention_gain, i...]
    reduce_sum x5 -> x0, other arithmetic: 8.49 us -> none  [the longest x2 3.24 us: norm_parts(): jnp.mean(values * values, axis=-1, keepdims=True) + norm_eps]
where the time goes in v1:
time: 470 us; the launch traced here: 462 us
  Pallas kernels  456 us (97%)
    pallas_call x1, Pallas kernels, run_experts(): pl.pallas_call(functools.partial(experts_kernel, experts), out_shape=(sha...  156 us
    pallas_call x1, Pallas kernels, begin(): pl.pallas_call(functools.partial(begin_kernel, heads), out_shape=(shape(*...  141 us
    pallas_call x1, Pallas kernels, end(): pl.pallas_call(functools.partial(end_kernel, heads), out_shape=(shape((co...  131 us
    pallas_call x1, Pallas kernels, expert_grads(): pl.pallas_call(expert_grads_kernel, grid=(steps,), in_specs=[pl.BlockSpec...  27.7 us

profile of v1, /device:TPU:16, one launch (start us, length us, event | category | flops | bytes accessed | tf_op | source)
XLA Modules:
  0.0 462.3 jit_solution(1801267134324183650)
XLA Ops:
  0.6 140.9 %begin.1 = (bf16[1,1024,2048]{2,1,0:T(8,128)(2,1)}, bf16[2048,512]{1,0:T(8,128)(2,1)}, bf16[2048,256]{1,0:T(8,128)(2,1)}, bf16[32,2048]{1,0:T(8,128)(2,1)}, s32[...) custom-call(bf16[2,128,2048]{2,1,0:T(8,128)(2,1)} %cot.3, ...), custom_call_target="tpu_custom_call" | custom-call | tf_op jit(solution)/shard_map/begin/pallas_call | solution.py:648
  141.5 156.3 %experts.1 = (bf16[2,1024,2048]{2,1,0:T(8,128)(2,1)}, bf16[3,2,1024,768]{3,2,1,0:T(8,128)(2,1)}, bf16[2,128,2048]{2,1,0:T(8,128)(2,1)}, bf16[2,128,2048]{2,1,0:T...) custom-call(bf16[2,128,2048]{2,1,0:T(8,128)(2,1)} %get-tuple-element.47.expert_in, ...), custom_call_target="tpu_custom_call" | custom-call | tf_op jit(solution)/shard_map/experts/pallas_call | solution.py:919
  297.8 130.7 %end.1 = (bf16[2,128,2048]{2,1,0:T(8,128)(2,1)}, bf16[2,128,2048]{2,1,0:T(8,128)(2,1)}, f32[256,1024]{1,0:T(8,128)}, f32[256,128]{1,0:T(8,128)}, f32[256,128]{1,...) custom-call(bf16[1,1024,2048]{2,1,0:T(8,128)(2,1)} %get-tuple-element.53.xn_in, ...), custom_call_target="tpu_custom_call" | custom-call | tf_op jit(solution)/shard_map/end/pallas_call | solution.py:1254
  428.6 0.0 copy-start.2
  428.6 0.0 copy-start.1
  428.6 0.0 copy-start
  428.6 27.7 %expert_grads.1 = (f32[768,2048]{1,0:T(8,128)}, f32[768,2048]{1,0:T(8,128)}, f32[768,2048]{1,0:T(8,128)}, bf16[2,128,2048]{2,1,0:T(8,128)(2,1)}, bf16[2,128,2048...) custom-call(bf16[3,2,1024,768]{3,2,1,0:T(8,128)(2,1)} %get-tuple-element.51.act, ...), custom_call_target="tpu_custom_call" | custom-call | tf_op jit(solution)/shard_map/expert_grads/pallas_call | solution.py:993
  456.3 0.0 copy-done.2
  456.3 0.6 slice_bitcast_fusion
  456.9 0.7 slice.19
  457.6 0.1 constant_dynamic-slice_fusion
  457.6 0.5 slice_bitcast_fusion.1
  458.2 0.7 slice.18
  458.9 1.3 dynamic-slice_divide_fusion
  460.2 0.6 slice.22
  460.7 0.0 copy-done.1
  460.7 0.7 copy.33
  461.4 0.0 copy-done
  461.4 0.7 copy.34
Async XLA Ops:
  428.6 27.7 %copy-start.2 = (f32[48,256]{1,0:T(8,128)S(1)}, f32[48,256]{1,0:T(8,128)}, u32[]{:S(2)}) copy-start(f32[48,256]{1,0:T(8,128)} %get-tuple-element.76) | copy-start | bytes 147460
  428.6 32.2 %copy-start.1 = (f32[256,128]{1,0:T(8,128)S(1)}, f32[256,128]{1,0:T(8,128)}, u32[]{:S(2)}) copy-start(f32[256,128]{1,0:T(8,128)} %get-tuple-element.102) | copy-start | bytes 393220
  428.6 32.8 %copy-start = (f32[256,128]{1,0:T(8,128)S(1)}, f32[256,128]{1,0:T(8,128)}, u32[]{:S(2)}) copy-start(f32[256,128]{1,0:T(8,128)} %get-tuple-element.103) | copy-start | bytes 393220

commit v2 on v1

--- a/solution.py
+++ b/solution.py
@@ -60,11 +60,16 @@
         return place(self.zr(d), (self.x + e) % 2, self.y, self.c)
 
     def greet(self):
-        barrier = pltpu.get_barrier_semaphore()
+        self.say()
+        self.hear()
+
+    def say(self):
         peers = [self.peer(d, e) for d in range(4) for e in range(2) if d or e] + [self.yn, self.cn]
         for peer in peers:
-            pl.semaphore_signal(barrier, inc=1, device_id=peer, device_id_type=MESH)
-        pl.semaphore_wait(barrier, len(peers))
+            pl.semaphore_signal(pltpu.get_barrier_semaphore(), inc=1, device_id=peer, device_id_type=MESH)
+
+    def hear(self):
+        pl.semaphore_wait(pltpu.get_barrier_semaphore(), 9)
 
 
 def remote(src, dst, send_sem, recv_sem, device):
@@ -503,6 +508,7 @@
                  cos_ref, sin_ref, qg_ref, kg_ref, xn_out, w_out, wo_out, router_out, ids_out, cot_out, pre_out, qkv_out, prob_out, ctx_out, resid_out, expert_out,
                  normed, resid, xn, w, wo, pre, qkv, prob, ctx, part, own, osem, *sems):
     here = Here()
+    here.say()
     count, rows, _ = tokens.shape
     step = 32
     steps = rows // step
@@ -515,7 +521,7 @@
         n, r = chunk_of(i)
         normed[n, r, :] = (unit(tokens[n, r, :].astype(F32))[0] * ag_ref[...]).astype(LOW)
 
-    here.greet()
+    here.hear()
     at = 0
     x_rows = Gather(here, False, normed, xn, sems[at : at + Gather.slots], BY_X)
     at += Gather.slots
@@ -887,10 +893,9 @@
     second = push(dgp_all, dgp_y, tsem.at[1], usem.at[1], here.yn)
     ahead.share_cross()
     behind.total()
-    behind.share_start()
+    quarter = keep(behind.tmp, out_sum, behind.osem.at[0])
     ahead.share_end(dx_sum)
-    behind.share_cross()
-    behind.share_end(out_sum)
+    quarter.wait()
     wait_for(dgp_y, usem.at[1], here.yn)
     dgp_out[...] = dgp_all[...] + dgp_y[...]
     second.wait_send()
@@ -922,7 +927,7 @@
             shape((count, seq, width), LOW),
             shape((3, count, seq, hidden), LOW),
             shape((count, rows, width), LOW),
-            shape((count, rows, width), LOW),
+            shape((count, rows, width // 4), LOW),
             shape((lanes, tokens), F32),
             shape((8, 8, tokens), F32),
         ),
@@ -1013,11 +1018,11 @@
                resid, cot, dx_sum, expert_in, probs, dgp, router, eg_ref, ag_ref, query, key, value,
                cos_ref, sin_ref, qg_ref, kg_ref,
                layer_out, input_out, dq_out, dk_out, dv_out, do_out, aux_out, gains_out,
-               tokens, out_sum, d_res, low_rows, layer, aux, db, xn, w, wo, pre, qkv, prob, ctx, dctx, dq_s, dk_s, dv_s, dqkv, dwo, dw, dwo_got, dwq_got, kv_x, kv_z,
+               tokens, out_full, d_res, low_rows, layer, aux, db, xn, w, wo, pre, qkv, prob, ctx, dctx, dq_s, dk_s, dv_s, dqkv, dwo, dw, dwo_got, dwq_got, kv_x, kv_z,
                aux_got, head_part, head_got, line, line_c, line_y, wide_q, wide_o, wide_kv,
-               lsem, psem, rsem, kxs, kxr, kzs, kzr, tsem, usem, osem, *rest):
+               lsem, psem, rsem, vsem, wsem, kxs, kxr, kzs, kzr, tsem, usem, osem, *rest):
     here = Here()
-    here.greet()
+    here.say()
     sends, outs = [], []
     rows_db = Gather(here, False, low_rows, db, rest[: Gather.slots], BY_X)
     at = Gather.slots
@@ -1041,7 +1046,7 @@
 
     loads = {}
     for n, (src, dst) in enumerate(((wo_in, wo), (ctx_in, ctx), (qkv_in, qkv), (prob_in, prob), (pre_in, pre),
-                                    (xn_in, xn), (w_in, w), (tokens_in, tokens), (out_in, out_sum))):
+                                    (xn_in, xn), (w_in, w), (tokens_in, tokens), (out_in, out_full.at[here.t]))):
         loads[n] = keep(src, dst, lsem.at[n])
     count, lanes, width = resid.shape[0], probs.shape[0], resid.shape[2]
     experts = lanes // 8
@@ -1071,6 +1076,7 @@
         return gain_part + jnp.sum(d_in * hat, axis=0, keepdims=True)
 
     gain_part = lax.fori_loop(0, count * steps, back, jnp.zeros((1, width), F32))
+    here.hear()
     rows_db.start()
     router_part = dot_nn(d_logits, expert_in[...].reshape(count * rows, width)).astype(LOW)
     first_row = lax.broadcasted_iota(jnp.int32, (16, piece), 0) == 0
@@ -1081,11 +1087,18 @@
     for d, e in PEERS:
         send(0, d, e, aux.at[number(d, e)], aux_got)
     rows_db.first_steps()
+    loads[8].wait()
+    mine = out_full.at[here.t]
+    sends.append(push(mine, mine, vsem.at[0], wsem.at[0], here.yn))
+    sends.append(push(mine, mine, vsem.at[1], wsem.at[1], here.cn))
     rows_db.last_steps()
     for d in (0,) + ORDER:
         rows_db.arrived(d, 0)
         rows_db.arrived(d, 1)
-    for n in range(9):
+    across = out_full.at[2 * (1 - here.y) + here.c]
+    wait_for(across, wsem.at[0], here.xn)
+    sends.append(push(across, across, vsem.at[2], wsem.at[2], here.cn))
+    for n in range(8):
         loads[n].wait()
 
     for i in range(seq // tile):
@@ -1096,10 +1109,14 @@
         dwo[r, :] = dot_tn(db[0, :, r], ctx[...]).astype(LOW)
         if d or e:
             send(1, d, e, dwo.at[r, :], dwo_got)
+    wait_for(out_full.at[2 * here.y + 1 - here.c], wsem.at[1], here.xn)
+    wait_for(out_full.at[2 * (1 - here.y) + 1 - here.c], wsem.at[2], here.xn)
+
     @pl.loop(0, count * steps)
     def _(i):
         n, r = chunk_of(i)
-        layer[n, r, :] = (resid[n, r, :] + out_sum[n, r, :].astype(F32)).astype(LOW)
+        routed = jnp.concatenate([out_full[q, n, r, :] for q in range(4)], axis=1).astype(F32)
+        layer[n, r, :] = (resid[n, r, :] + routed).astype(LOW)
 
     outs.append(keep(layer, layer_out, osem.at[4]))
     dk_s[...] = jnp.zeros_like(dk_s)
@@ -1151,7 +1168,7 @@
     for d, e in PEERS + ((0, 0),):
         r = span(number(d, e) * piece, piece)
         dw[r, :] = dot_tn(xn[0, :, r], dqkv[...]).astype(LOW)
-        if d or e:
+        if d in (1, 2):
             send(2, d, e, dw.at[r, pl.ds(0, part)], dwq_got)
         if e:
             sends.append(push(dw.at[r, pl.ds(part, 2 * hd)], kv_x.at[d], kxs.at[d], kxr.at[d], here.xn))
@@ -1169,6 +1186,9 @@
         dn.sides(d)
     for d in FAR_FIRST:
         dn.centre(d)
+    for d, e in PEERS:
+        if d in (0, 3):
+            send(2, d, e, dw.at[span(number(d, e) * piece, piece), pl.ds(0, part)], dwq_got)
 
     def merged(n, wide, got, mine):
         for d in (0, 1):
@@ -1267,7 +1287,7 @@
         out_specs=[hbm] * 6 + [near] * 2,
         scratch_shapes=[
             vm((count, rows, width), LOW),
-            vm((count, rows, width), LOW),
+            vm((4, count, rows, width // 4), LOW),
             vm((count, rows, width), F32),
             vm((count, rows, width), LOW),
             vm((count, rows, width), LOW),
@@ -1303,6 +1323,8 @@
             dma((9,)),
             dma((4, 4, 2)),
             dma((4, 4, 2)),
+            dma((3,)),
+            dma((3,)),
             dma((4,)),
             dma((4,)),
             dma((4,)),

time: 470 us -> 461 us (0.981)
  Pallas kernels: 456 us -> 447 us
    pallas_call x1, Pallas kernels: 131 us -> 126 us  [end(): pl.pallas_call(functools.partial(end_kernel, heads), out_shape=(shape((co...]
where the time goes in v2:
time: 461 us; the launch traced here: 454 us
  Pallas kernels  447 us (97%)
    pallas_call x1, Pallas kernels, run_experts(): pl.pallas_call(functools.partial(experts_kernel, experts), out_shape=(sha...  154 us
    pallas_call x1, Pallas kernels, begin(): pl.pallas_call(functools.partial(begin_kernel, heads), out_shape=(shape(*...  140 us
    pallas_call x1, Pallas kernels, end(): pl.pallas_call(functools.partial(end_kernel, heads), out_shape=(shape((co...  126 us
    pallas_call x1, Pallas kernels, expert_grads(): pl.pallas_call(expert_grads_kernel, grid=(steps,), in_specs=[pl.BlockSpec...  27.7 us

profile of v2, /device:TPU:16, one launch (start us, length us, event | category | flops | bytes accessed | tf_op | source)
XLA Modules:
  0.0 453.9 jit_solution(2753868920377301336)
XLA Ops:
  0.6 139.7 %begin.1 = (bf16[1,1024,2048]{2,1,0:T(8,128)(2,1)}, bf16[2048,512]{1,0:T(8,128)(2,1)}, bf16[2048,256]{1,0:T(8,128)(2,1)}, bf16[32,2048]{1,0:T(8,128)(2,1)}, s32[...) custom-call(bf16[2,128,2048]{2,1,0:T(8,128)(2,1)} %cot.3, ...), custom_call_target="tpu_custom_call" | custom-call | tf_op jit(solution)/shard_map/begin/pallas_call | solution.py:654
  140.4 154.3 %experts.1 = (bf16[2,1024,2048]{2,1,0:T(8,128)(2,1)}, bf16[3,2,1024,768]{3,2,1,0:T(8,128)(2,1)}, bf16[2,128,2048]{2,1,0:T(8,128)(2,1)}, bf16[2,128,512]{2,1,0:T(...) custom-call(bf16[2,128,2048]{2,1,0:T(8,128)(2,1)} %get-tuple-element.47.expert_in, ...), custom_call_target="tpu_custom_call" | custom-call | tf_op jit(solution)/shard_map/experts/pallas_call | solution.py:924
  294.6 125.5 %end.1 = (bf16[2,128,2048]{2,1,0:T(8,128)(2,1)}, bf16[2,128,2048]{2,1,0:T(8,128)(2,1)}, f32[256,1024]{1,0:T(8,128)}, f32[256,128]{1,0:T(8,128)}, f32[256,128]{1,...) custom-call(bf16[1,1024,2048]{2,1,0:T(8,128)(2,1)} %get-tuple-element.53.xn_in, ...), custom_call_target="tpu_custom_call" | custom-call | tf_op jit(solution)/shard_map/end/pallas_call | solution.py:1274
  420.2 0.0 copy-start.2
  420.2 0.0 copy-start.1
  420.2 0.0 copy-start
  420.2 27.7 %expert_grads.1 = (f32[768,2048]{1,0:T(8,128)}, f32[768,2048]{1,0:T(8,128)}, f32[768,2048]{1,0:T(8,128)}, bf16[2,128,2048]{2,1,0:T(8,128)(2,1)}, bf16[2,128,2048...) custom-call(bf16[3,2,1024,768]{3,2,1,0:T(8,128)(2,1)} %get-tuple-element.51.act, ...), custom_call_target="tpu_custom_call" | custom-call | tf_op jit(solution)/shard_map/expert_grads/pallas_call | solution.py:998
  447.8 0.0 copy-done.2
  447.8 0.6 slice_bitcast_fusion
  448.5 0.7 slice.19
  449.1 0.1 constant_dynamic-slice_fusion
  449.2 0.5 slice_bitcast_fusion.1
  449.7 0.7 slice.18
  450.4 1.3 dynamic-slice_divide_fusion
  451.8 0.6 slice.22
  452.3 0.0 copy-done.1
  452.3 0.7 copy.33
  453.0 0.0 copy-done
  453.0 0.7 copy.34
Async XLA Ops:
  420.2 27.7 %copy-start.2 = (f32[48,256]{1,0:T(8,128)S(1)}, f32[48,256]{1,0:T(8,128)}, u32[]{:S(2)}) copy-start(f32[48,256]{1,0:T(8,128)} %get-tuple-element.76) | copy-start | bytes 147460
  420.2 32.2 %copy-start.1 = (f32[256,128]{1,0:T(8,128)S(1)}, f32[256,128]{1,0:T(8,128)}, u32[]{:S(2)}) copy-start(f32[256,128]{1,0:T(8,128)} %get-tuple-element.102) | copy-start | bytes 393220
  420.2 32.8 %copy-start = (f32[256,128]{1,0:T(8,128)S(1)}, f32[256,128]{1,0:T(8,128)}, u32[]{:S(2)}) copy-start(f32[256,128]{1,0:T(8,128)} %get-tuple-element.103) | copy-start | bytes 393220

commit v3 on v2

--- a/solution.py
+++ b/solution.py
@@ -686,7 +686,8 @@
                    x_t, g, u, dn, og_t, raw_s, act_t, dx, out, stage, share_s, dgp_t, dgp_got, dgp_all, dgp_c, dgp_y,
                    wsem, ogsem, xsem, actsem, psem, rsem, tsem, usem, *rest):
     here = Here()
-    here.greet()
+    here.say()
+    loads = [keep(src, dst, wsem.at[n]) for n, (src, dst) in enumerate(((d_in, dn), (g_in, g), (u_in, u)))]
     by_x = expert_in.shape[1] // 2
     rows_x = Gather(here, True, expert_in, x_out, rest[: Gather.slots], by_x, x_t.at[0])
     sums = (
@@ -701,8 +702,8 @@
     lanes = router.shape[0]
     part = stage.shape[2]
     chunk = width // 4
+    here.hear()
     rows_x.start()
-    loads = [keep(src, dst, wsem.at[n]) for n, (src, dst) in enumerate(((d_in, dn), (g_in, g), (u_in, u)))]
 
     def plane(i):
         k = i // 2
@@ -1867,8 +1868,8 @@
         query_gain,
         key_gain,
     )
-    d_gate, d_up, d_down, layer_output, input_grad, d_query, d_output = expert_grads(
-        act, expert_all, grad_all, layer_output, input_grad, d_query, d_output
+    d_gate, d_up, d_down, layer_output, input_grad, d_query, d_output, d_key, d_value = expert_grads(
+        act, expert_all, grad_all, layer_output, input_grad, d_query, d_output, d_key, d_value
     )
     own_gain = lax.dynamic_slice_in_dim(attention_gain, f * piece, piece, 0)
     head_piece = hd // n_fsdp

time: 461 us -> 459 us (level)
  no operation moved by 1% of the time
where the time goes in v3:
time: 459 us; the launch traced here: 451 us
  Pallas kernels  446 us (97%)
    pallas_call x1, Pallas kernels, run_experts(): pl.pallas_call(functools.partial(experts_kernel, experts), out_shape=(sha...  154 us
    pallas_call x1, Pallas kernels, begin(): pl.pallas_call(functools.partial(begin_kernel, heads), out_shape=(shape(*...  140 us
    pallas_call x1, Pallas kernels, end(): pl.pallas_call(functools.partial(end_kernel, heads), out_shape=(shape((co...  123 us
    pallas_call x1, Pallas kernels, expert_grads(): pl.pallas_call(expert_grads_kernel, grid=(steps,), in_specs=[pl.BlockSpec...  28.2 us

profile of v3, /device:TPU:16, one launch (start us, length us, event | category | flops | bytes accessed | tf_op | source)
XLA Modules:
  0.0 451.1 jit_solution(6084718959703785567)
XLA Ops:
  0.6 139.7 %begin.1 = (bf16[1,1024,2048]{2,1,0:T(8,128)(2,1)}, bf16[2048,512]{1,0:T(8,128)(2,1)}, bf16[2048,256]{1,0:T(8,128)(2,1)}, bf16[32,2048]{1,0:T(8,128)(2,1)}, s32[...) custom-call(bf16[2,128,2048]{2,1,0:T(8,128)(2,1)} %cot.3, ...), custom_call_target="tpu_custom_call" | custom-call | tf_op jit(solution)/shard_map/begin/pallas_call | solution.py:654
  140.4 154.4 %experts.1 = (bf16[2,1024,2048]{2,1,0:T(8,128)(2,1)}, bf16[3,2,1024,768]{3,2,1,0:T(8,128)(2,1)}, bf16[2,128,2048]{2,1,0:T(8,128)(2,1)}, bf16[2,128,512]{2,1,0:T(...) custom-call(bf16[2,128,2048]{2,1,0:T(8,128)(2,1)} %get-tuple-element.49.expert_in, ...), custom_call_target="tpu_custom_call" | custom-call | tf_op jit(solution)/shard_map/experts/pallas_call | solution.py:925
  294.8 123.4 %end.1 = (bf16[2,128,2048]{2,1,0:T(8,128)(2,1)}, bf16[2,128,2048]{2,1,0:T(8,128)(2,1)}, f32[256,1024]{1,0:T(8,128)}, f32[256,128]{1,0:T(8,128)}, f32[256,128]{1,...) custom-call(bf16[1,1024,2048]{2,1,0:T(8,128)(2,1)} %get-tuple-element.55.xn_in, ...), custom_call_target="tpu_custom_call" | custom-call | tf_op jit(solution)/shard_map/end/pallas_call | solution.py:1275
  418.2 0.0 copy-start
  418.2 28.2 %expert_grads.1 = (f32[768,2048]{1,0:T(8,128)}, f32[768,2048]{1,0:T(8,128)}, f32[768,2048]{1,0:T(8,128)}, bf16[2,128,2048]{2,1,0:T(8,128)(2,1)}, bf16[2,128,2048...) custom-call(bf16[3,2,1024,768]{3,2,1,0:T(8,128)(2,1)} %get-tuple-ele, ...), custom_call_target="tpu_custom_call" | custom-call | tf_op jit(solution)/shard_map/expert_grads/pallas_call | solution.py:999
  446.4 0.0 copy-done
  446.4 0.6 slice_bitcast_fusion
  447.1 0.7 slice.19
  447.7 0.1 constant_dynamic-slice_fusion
  447.8 0.5 slice_bitcast_fusion.1
  448.3 0.7 slice.18
  449.0 1.3 dynamic-slice_divide_fusion
  450.3 0.6 slice.22
Async XLA Ops:
  418.2 28.2 %copy-start = (f32[48,256]{1,0:T(8,128)S(1)}, f32[48,256]{1,0:T(8,128)}, u32[]{:S(2)}) copy-start(f32[48,256]{1,0:T(8,128)} %get-tuple-element.80) | copy-start | bytes 147460
